TPU v7x, 256 devices: a whole 4x4x8 slice. The times are simulated.
256 devices in a mesh: gx: 64 (over z_hi, x, y), gy: 4 (over z_lo, core).
Axes of the slice: x: 4, y: 4, z: 8 (z_hi: 4, z_lo: 2; z = z_hi * 2 + z_lo), core: 2. Of those that a mesh axis runs over, the one named last changes fastest.
Arguments:
- density: float32 [4096, 32768], P('gx', 'gy'), may hold values from -6 to 6
- kz_square: float32 [8], replicated, may hold values from 0.25 to 4
Outputs:
- potential: float32 [2, 2048, 8, 4096], P(None, ('gx', 'gy'))
All inputs are finite; a program needn't handle non-finite values.
Results may differ from a plain program's by a relative error of at most 0.000071.
Values sent between devices are 32-bit elements; how exact they have to be, the bound alone decides.
No kernel may reach another device: no remote copies, remote signals or barrier semaphores. Data moves between devices by JAX's collectives and lax.ppermute only.
A program may use at most 64 MiB of HBM per device.

v0:
```python
import functools
import math

import jax
import jax.numpy as jnp
import ml_dtypes
import numpy as np
from jax import lax
from jax.experimental import pallas as pl
from jax.experimental.pallas import tpu as pltpu
from jax.sharding import Mesh
from jax.sharding import PartitionSpec as P

LENGTH = 4096
KEPT = 2048
ROOT = 64
LANES = 128
HALF = 64
PLANES = 8
AXES = ("zh", "x", "y", "zl", "core")


def split_table(table, axis, order):
    high = table.astype(ml_dtypes.bfloat16)
    low = (table - high.astype(np.float64)).astype(ml_dtypes.bfloat16)
    parts = {"h": high, "l": low}
    return np.concatenate([parts[name] for name in order], axis=axis)


def split_data(values, axis, order):
    high = values.astype(jnp.bfloat16)
    low = (values - high.astype(jnp.float32)).astype(jnp.bfloat16)
    parts = {"h": high, "l": low}
    return jnp.concatenate([parts[name] for name in order], axis=axis)


@functools.cache
def x_tables():
    a = np.arange(ROOT)
    first = 2.0 * np.pi * np.outer(np.arange(ROOT // 2 + 1), a) / ROOT
    outer = np.concatenate([np.cos(first), -np.sin(first[1 : ROOT // 2])], axis=0)
    sections = []
    k2 = np.arange(KEPT // ROOT)
    for k1 in range(ROOT // 2 + 1):
        angle = 2.0 * np.pi * np.outer(k1 + ROOT * k2, a) / LENGTH
        rows = [np.concatenate([np.cos(angle), -np.sin(angle)], axis=1)]
        mirror = 2.0 * np.pi * np.outer((ROOT - k1) % ROOT + ROOT * k2, a) / LENGTH
        rows.append(np.concatenate([np.cos(mirror), np.sin(mirror)], axis=1))
        sections.append(np.concatenate(rows, axis=0))
    return split_table(outer, 1, "hhl"), split_table(np.stack(sections), 2, "hhl")


@functools.cache
def y_tables():
    source = np.arange(256)
    place = (source % 4) * 64 + source // 4
    angle = 2.0 * np.pi * np.outer(place, np.arange(256)) / 256
    table = np.concatenate([np.cos(angle), -np.sin(angle)], axis=1)
    turn = 2.0 * np.pi * np.outer(np.arange(16), np.arange(256)) / LENGTH
    wave = np.arange(LENGTH).reshape(16, 256)
    symbol = 4.0 * np.sin(np.pi * wave / LENGTH) ** 2
    return (
        split_table(table, 0, "hhl"),
        np.cos(turn).astype(np.float32),
        (-np.sin(turn)).astype(np.float32),
        symbol.astype(np.float32),
    )


def x_kernel(outer_ref, section_ref, lines_ref, out_ref, mixed_ref):
    outer = outer_ref[...]
    for b in range(0, ROOT, 2):
        pair = jnp.concatenate(
            [lines_ref[pl.ds(b + i, ROOT, stride=ROOT), :] for i in range(2)], axis=1
        )
        mixed = jnp.dot(outer, split_data(pair, 0, "hlh"), preferred_element_type=jnp.float32)
        for i in range(2):
            mixed_ref[pl.ds(b + i, ROOT, stride=ROOT), :] = mixed[:, i * LANES : (i + 1) * LANES]
    left = lax.broadcasted_iota(jnp.int32, (ROOT, LANES), 1) < HALF
    keep = lax.broadcasted_iota(jnp.int32, (KEPT // ROOT, 2 * LANES), 1) % LANES < HALF
    for k1 in range(ROOT // 2 + 1):
        real = mixed_ref[k1 * ROOT : (k1 + 1) * ROOT, :]
        real_turned = pltpu.roll(real, HALF, 1)
        if 0 < k1 < ROOT // 2:
            imag = mixed_ref[(ROOT // 2 + k1) * ROOT : (ROOT // 2 + k1 + 1) * ROOT, :]
            imag_turned = pltpu.roll(imag, HALF, 1)
        else:
            imag = jnp.zeros_like(real)
            imag_turned = imag
        upper = jnp.concatenate(
            [jnp.where(left, real, imag_turned), jnp.where(left, real_turned, imag)], axis=1
        )
        lower = jnp.concatenate(
            [jnp.where(left, -imag, real_turned), jnp.where(left, -imag_turned, real)], axis=1
        )
        data = split_data(jnp.concatenate([upper, lower], axis=0), 0, "hlh")
        result = jnp.dot(section_ref[k1], data, preferred_element_type=jnp.float32)
        count = KEPT // ROOT
        for h in range(2):
            start = (k1 // 8) * 16 + h * 8 + k1 % 8
            out_ref[pl.ds(start, count, stride=LANES), :] = result[:count, h * LANES : (h + 1) * LANES]
        if 0 < k1 < ROOT // 2:
            other = ROOT - k1
            mirrored = jnp.where(keep, result[count:], -result[count:])
            for h in range(2):
                start = (other // 8) * 16 + h * 8 + other % 8
                out_ref[pl.ds(start, count, stride=LANES), :] = mirrored[:, h * LANES : (h + 1) * LANES]


def x_transform(lines):
    outer, sections = x_tables()
    return pl.pallas_call(
        x_kernel,
        out_shape=jax.ShapeDtypeStruct((LENGTH, LANES), jnp.float32),
        scratch_shapes=[pltpu.VMEM((LENGTH, LANES), jnp.float32)],
        compiler_params=pltpu.CompilerParams(vmem_limit_bytes=40 << 20),
        name="x_transform",
    )(jnp.asarray(outer), jnp.asarray(sections), lines)


def add(p, q):
    return (p[0] + q[0], p[1] + q[1])


def sub(p, q):
    return (p[0] - q[0], p[1] - q[1])


def turn_back(p):
    return (p[1], -p[0])


def times(p, angle):
    cosine, sine_part = math.cos(angle), math.sin(angle)
    return (p[0] * cosine - p[1] * sine_part, p[1] * cosine + p[0] * sine_part)


def four(p, q, r, s):
    even, odd = add(p, r), add(q, s)
    even_minus, odd_minus = sub(p, r), turn_back(sub(q, s))
    return add(even, odd), add(even_minus, odd_minus), sub(even, odd), sub(even_minus, odd_minus)


def sixteen(values):
    columns = []
    for n in range(4):
        column = four(*[values[4 * m + n] for m in range(4)])
        columns.append([times(v, -2.0 * math.pi * n * k / 16) if n * k else v for k, v in enumerate(column)])
    out = [None] * 16
    for k in range(4):
        for l, v in enumerate(four(*[columns[n][k] for n in range(4)])):
            out[k + 4 * l] = v
    return out


def y_kernel(symbol_x_ref, table_ref, cosine_ref, sine_ref, symbol_ref, kz_ref, lines_ref, out_ref):
    table = table_ref[...]
    scale = -1.0 / math.sqrt(LENGTH * LENGTH)
    kz = kz_ref[...]
    for j in range(8):
        rows = []
        for h in range(2):
            values = lines_ref[pl.ds(h * 8 + j, 256, stride=16), :]
            rows.append(split_data(values.T, 1, "hlh"))
        product = jnp.dot(jnp.concatenate(rows, axis=0), table, preferred_element_type=jnp.float32)
        values = []
        for h in range(2):
            for m in range(8):
                first = product[h * LANES + m * 8 : h * LANES + m * 8 + 8]
                second = product[h * LANES + HALF + m * 8 : h * LANES + HALF + m * 8 + 8]
                real = first[:, :256] - second[:, 256:]
                imag = first[:, 256:] + second[:, :256]
                n = h * 8 + m
                if n:
                    cosine, sine_part = cosine_ref[n : n + 1, :], sine_ref[n : n + 1, :]
                    real, imag = real * cosine - imag * sine_part, imag * cosine + real * sine_part
                values.append((real, imag))
        shift = kz + symbol_x_ref[j]
        for k, (real, imag) in enumerate(sixteen(values)):
            factor = scale / (shift + symbol_ref[k : k + 1, :])
            out_ref[0, j, :, k * 256 : (k + 1) * 256] = real * factor
            out_ref[1, j, :, k * 256 : (k + 1) * 256] = imag * factor


def y_transform(lines, symbol_x, kz_square):
    table, cosine, sine_part, symbol = y_tables()
    vmem = pl.BlockSpec(memory_space=pltpu.VMEM)
    return pl.pallas_call(
        y_kernel,
        out_shape=jax.ShapeDtypeStruct((2, 8, PLANES, LENGTH), jnp.float32),
        in_specs=[pl.BlockSpec(memory_space=pltpu.SMEM)] + [vmem] * 6,
        compiler_params=pltpu.CompilerParams(vmem_limit_bytes=40 << 20),
        name="y_transform",
    )(
        symbol_x,
        jnp.asarray(table),
        jnp.asarray(cosine),
        jnp.asarray(sine_part),
        jnp.asarray(symbol),
        jnp.broadcast_to(kz_square[:, None], (PLANES, 256)),
        lines,
    )


def body(density, kz_square):
    gx = AXES[:3]
    blocks = jnp.transpose(density.reshape(64, 64, LANES), (1, 0, 2))
    lines = lax.all_to_all(blocks, gx, 0, 0, tiled=True)
    spectrum = x_transform(lines.reshape(LENGTH, LANES))
    lines = lax.all_to_all(spectrum.reshape(256, 16, LANES), AXES, 0, 0, tiled=True)
    wave_x = (lax.axis_index(AXES) * 8 + jnp.arange(8, dtype=jnp.int32)).astype(jnp.float32)
    symbol_x = 4.0 * jnp.sin(wave_x * (math.pi / LENGTH)) ** 2
    return y_transform(lines.reshape(LENGTH, LANES), symbol_x, kz_square)


def solution(mesh):
    fine = Mesh(mesh.devices.reshape(4, 4, 4, 2, 2), AXES)
    in_specs = (P(AXES[:3], AXES[3:]), P())
    out_specs = P(None, AXES, None, None)
    return jax.shard_map(body, mesh=fine, in_specs=in_specs, out_specs=out_specs, check_vma=False)
```

profile of v0, /device:TPU:1, one launch (start us, length us, event | category | flops | bytes accessed | tf_op | source)
XLA Modules:
  0.0 142.5 jit_solution(4498501123985261926)
XLA Ops:
  0.0 0.0 copy-start
  0.0 1.6 %copy-done = f32[64,8192]{1,0:T(8,128)S(1)} copy-done((f32[64,8192]{1,0:T(8,128)S(1)}, f32[64,8192]{1,0:T(8,128)}, u32[]{:S(2)}) %copy-start) | copy-done | bytes 2097176
  1.6 0.3 bitcast_bitcast_fusion
  1.9 0.0 copy-start.2
  1.9 0.0 copy-start.4
  1.9 62.1 %all_to_all.10 = f32[64,64,128]{2,1,0:T(8,128)S(1)} all-to-all(f32[64,64,128]{2,1,0:T(8,128)S(1)} %bitcast_bitcast_fusion), channel_id=1, replica_groups=mesh['zh'=4,'x'=4,'y'=4,'zl'=2,'core'=2] {'zh','x','y'}, dimensions={0} | all-to-all | bytes 4194304 | tf_op jit(solution)/shard_map/all_to_all | solution.py:208
  64.0 0.0 copy-done.2
  64.0 0.0 copy-done.4
  64.0 4.7 %x_transform.1 = f32[4096,128]{1,0:T(8,128)S(1)} custom-call(bf16[64,192]{1,0:T(8,128)(2,1)S(1)} %copy-done.4, bf16[33,64,384]{2,1,0:T(8,128)(2,1)S(1)} %copy-done.2, f32[4096,128]{1,0:T(8,128)S(1)} %bitcast.11), custom_call_target="tpu_custom_call" | custom-call | tf_op jit(solution)/shard_map/x_transform/pallas_call | solution.py:112
  68.7 0.0 copy-start.1
  68.7 1.3 copy-done.1
  70.0 0.0 copy-start.8
  70.0 0.0 copy-start.3
  70.0 0.0 copy-start.5
  70.0 0.0 copy-start.7
  70.1 13.3 %all-to-all-start.1 = ((f32[256,16,128]{2,1,0:T(8,128)}), f32[256,16,128]{2,1,0:T(8,128)}, u32[]{:S(2)}, u32[]{:S(2)}) async-start(f32[256,16,128]{2,1,0:T(8,128)} %bitcast.10), calls=%async_computation.1 | async-start | bytes 4194304 | tf_op jit(solution)/shard_map/all_to_all | solution.py:210
  83.4 53.7 %all-to-all-done.1 = f32[256,16,128]{2,1,0:T(8,128)} async-done(((f32[256,16,128]{2,1,0:T(8,128)}), f32[256,16,128]{2,1,0:T(8,128)}, u32[]{:S(2)}, u32[]{:S(2)}) %all-to-all-start.1) | async-done | bytes 2097184 | tf_op jit(solution)/shard_map/all_to_all | solution.py:210
  137.1 0.0 copy-done.8
  137.1 0.1 broadcast_in_dim.2.kz_ref
  137.2 0.0 copy-done.3
  137.2 0.0 copy-done.5
  137.2 0.0 copy-done.6
  137.2 0.0 copy-done.7
  137.2 5.3 %y_transform.1 = f32[2,8,8,4096]{3,2,1,0:T(8,128)} custom-call(f32[8]{0:T(128)S(1)} %multiply_multiply_fusion.symbol_x_ref, bf16[768,512]{1,0:T(8,128)(2,1)S(1)} %copy-done.3, f32[16,256]{1,0:T(8,128)S(1)} %copy-done.5, f32[16,256]{1,0:T(8,128)S(1)} %copy-done.6, f32[16,256]{1,0:T(8,128)S(1)} %copy-done.7, f32[8,256]{1,0:T(8,128)S(1)} %broadcast_in_dim.2.kz_ref, ...), custom_call_target="tpu_custom_call" | custom-call | tf_op jit(solution)/shard_map/y_transform/pallas_call | solution.py:188
  (2 shorter events, 0.0 us)
Async XLA Ops:
  0.0 1.6 %copy-start = (f32[64,8192]{1,0:T(8,128)S(1)}, f32[64,8192]{1,0:T(8,128)}, u32[]{:S(2)}) copy-start(f32[64,8192]{1,0:T(8,128)} %param.8) | copy-start | bytes 6291460
  1.9 62.1 %copy-start.2 = (bf16[33,64,384]{2,1,0:T(8,128)(2,1)S(1)}, bf16[33,64,384]{2,1,0:T(8,128)(2,1)}, u32[]{:S(2)}) copy-start(bf16[33,64,384]{2,1,0:T(8,128)(2,1)} %constant.46.clone.section_ref) | copy-start | bytes 4866052
  1.9 62.1 %copy-start.4 = (bf16[64,192]{1,0:T(8,128)(2,1)S(1)}, bf16[64,192]{1,0:T(8,128)(2,1)}, u32[]{:S(2)}) copy-start(bf16[64,192]{1,0:T(8,128)(2,1)} %constant.45.clone.outer_ref) | copy-start | bytes 73732
  68.7 1.3 copy-start.1
  70.0 67.1 %copy-start.8 = (f32[8]{0:T(128)S(1)}, f32[8]{0:T(128)}, u32[]{:S(2)}) copy-start(f32[8]{0:T(128)} %param.9) | copy-start | bytes 100
  70.0 67.1 %copy-start.3 = (bf16[768,512]{1,0:T(8,128)(2,1)S(1)}, bf16[768,512]{1,0:T(8,128)(2,1)}, u32[]{:S(2)}) copy-start(bf16[768,512]{1,0:T(8,128)(2,1)} %constant.47.clone.table_ref) | copy-start | bytes 2359300
  70.0 67.2 %copy-start.5 = (f32[16,256]{1,0:T(8,128)S(1)}, f32[16,256]{1,0:T(8,128)}, u32[]{:S(2)}) copy-start(f32[16,256]{1,0:T(8,128)} %constant.48.clone.cosine_ref) | copy-start | bytes 49156
  70.0 67.2 %copy-start.6 = (f32[16,256]{1,0:T(8,128)S(1)}, f32[16,256]{1,0:T(8,128)}, u32[]{:S(2)}) copy-start(f32[16,256]{1,0:T(8,128)} %constant.49.clone.sine_ref) | copy-start | bytes 49156
  70.0 67.1 %copy-start.7 = (f32[16,256]{1,0:T(8,128)S(1)}, f32[16,256]{1,0:T(8,128)}, u32[]{:S(2)}) copy-start(f32[16,256]{1,0:T(8,128)} %constant.50.clone.symbol_ref) | copy-start | bytes 49156
  70.1 67.1 %all-to-all-start.1 = ((f32[256,16,128]{2,1,0:T(8,128)}), f32[256,16,128]{2,1,0:T(8,128)}, u32[]{:S(2)}, u32[]{:S(2)}) async-start(f32[256,16,128]{2,1,0:T(8,128)} %bitcast.10), calls=%async_computation.1 | async-start | bytes 4194304 | tf_op jit(solution)/shard_map/all_to_all | solution.py:210
where the time goes:
time: 143 us; the launch traced here: 142 us
  blocking collectives  62.1 us (43%)
  waiting for transfers between devices  53.7 us (38%)
  starting transfers between devices  13.3 us (9%)
  Pallas kernels  9.99 us (7%)
  local copies, waits for them, and re-layouts  3.27 us (2%)
    all_to_all x1, blocking collectives, body(): lines = lax.all_to_all(blocks, gx, 0, 0, tiled=True)  62.1 us
    all_to_all x1, waiting for transfers between devices, body(): lax.all_to_all(spectrum.reshape(256, 16, LANES), AXES, 0, 0, tiled=True)  53.7 us
    all_to_all x1, starting transfers between devices, body(): lax.all_to_all(spectrum.reshape(256, 16, LANES), AXES, 0, 0, tiled=True)  13.3 us
    pallas_call x1, Pallas kernels, y_transform(): pl.pallas_call(y_kernel, out_shape=jax.ShapeDtypeStruct((2, 8, PLANES, LE...  5.27 us
    pallas_call x1, Pallas kernels, x_transform(): pl.pallas_call(x_kernel, out_shape=jax.ShapeDtypeStruct((LENGTH, LANES),...  4.72 us
    unnamed x18, local copies, waits for them, and re-layouts  2.94 us
  transfers between devices with their start and end apart: 1, of which 1 were waited for; matrix products, arithmetic and copies ran while one was open for 0% of the time, Pallas kernels for 0%

commit v1 on v0

--- a/solution.py
+++ b/solution.py
@@ -17,6 +17,8 @@
 LANES = 128
 HALF = 64
 PLANES = 8
+ROWS = 32
+SLOT = 256
 AXES = ("zh", "x", "y", "zl", "core")
 
 
@@ -53,7 +55,8 @@
 @functools.cache
 def y_tables():
     source = np.arange(256)
-    place = (source % 4) * 64 + source // 4
+    zh, zl, xy, core = source // 64, source // 32 % 2, source // 2 % 16, source % 2
+    place = (zl * 2 + core) * 64 + zh * 16 + xy
     angle = 2.0 * np.pi * np.outer(place, np.arange(256)) / 256
     table = np.concatenate([np.cos(angle), -np.sin(angle)], axis=1)
     turn = 2.0 * np.pi * np.outer(np.arange(16), np.arange(256)) / LENGTH
@@ -67,55 +70,152 @@
     )
 
 
-def x_kernel(outer_ref, section_ref, lines_ref, out_ref, mixed_ref):
-    outer = outer_ref[...]
-    for b in range(0, ROOT, 2):
-        pair = jnp.concatenate(
-            [lines_ref[pl.ds(b + i, ROOT, stride=ROOT), :] for i in range(2)], axis=1
-        )
+def left_lanes(rows):
+    return lax.broadcasted_iota(jnp.int32, (rows, LANES), 1) < HALF
+
+
+def pack_kernel(place_ref, density_ref, *out_refs):
+    zh = place_ref[0]
+    left = left_lanes(ROWS)
+    for dz in range(4):
+        base = ((zh + dz) & 3) * (16 * LANES)
+        for xy in range(16):
+            start = pl.multiple_of(base + xy * LANES, LANES)
+            upper = density_ref[:ROWS, pl.ds(start, LANES)]
+            lower = density_ref[ROWS:, pl.ds(start, LANES)]
+            out_refs[dz][xy] = jnp.where(left, upper, pltpu.roll(lower, HALF, 1))
+            out_refs[4][xy, dz] = jnp.where(left, pltpu.roll(upper, HALF, 1), lower)
+
+
+def join_kernel(*refs):
+    for slot, ref in enumerate(refs[:-1]):
+        refs[-1][:, slot] = ref[...]
+
+
+def split_kernel(in_ref, *out_refs):
+    for slot, ref in enumerate(out_refs):
+        ref[...] = in_ref[:, slot]
+
+
+def call(kernel, name, out_shape, scalars, *arrays, scratch=()):
+    vmem = pl.BlockSpec(memory_space=pltpu.VMEM)
+    smem = pl.BlockSpec(memory_space=pltpu.SMEM)
+    return pl.pallas_call(
+        kernel,
+        out_shape=out_shape,
+        in_specs=[smem] * len(scalars) + [vmem] * len(arrays),
+        scratch_shapes=list(scratch),
+        compiler_params=pltpu.CompilerParams(vmem_limit_bytes=40 << 20),
+        name=name,
+    )(*scalars, *arrays)
+
+
+def floats(*shape):
+    return jax.ShapeDtypeStruct(shape, jnp.float32)
+
+
+def pack(density, place):
+    out_shape = [floats(16, ROWS, LANES)] * 4 + [floats(16, 4, ROWS, LANES)]
+    return call(pack_kernel, "pack", out_shape, [place], density)
+
+
+def join(parts):
+    n, rows, lanes = parts[0].shape
+    return call(join_kernel, "join", floats(n, len(parts), rows, lanes), [], *parts)
+
+
+def split(whole):
+    n, count, rows, lanes = whole.shape
+    return call(split_kernel, "split", [floats(n, rows, lanes)] * count, [], whole)
+
+
+def x_steps(outer, section_ref, load_row, mixed_ref, store):
+    for r in range(0, ROWS, 2):
+        pair = jnp.concatenate([load_row(r), load_row(r + 1)], axis=1)
         mixed = jnp.dot(outer, split_data(pair, 0, "hlh"), preferred_element_type=jnp.float32)
         for i in range(2):
-            mixed_ref[pl.ds(b + i, ROOT, stride=ROOT), :] = mixed[:, i * LANES : (i + 1) * LANES]
-    left = lax.broadcasted_iota(jnp.int32, (ROOT, LANES), 1) < HALF
-    keep = lax.broadcasted_iota(jnp.int32, (KEPT // ROOT, 2 * LANES), 1) % LANES < HALF
+            mixed_ref[pl.ds(r + i, ROOT, stride=ROWS), :] = mixed[:, i * LANES : (i + 1) * LANES]
+    left = left_lanes(ROWS)
     for k1 in range(ROOT // 2 + 1):
-        real = mixed_ref[k1 * ROOT : (k1 + 1) * ROOT, :]
+        real = mixed_ref[k1 * ROWS : (k1 + 1) * ROWS, :]
         real_turned = pltpu.roll(real, HALF, 1)
         if 0 < k1 < ROOT // 2:
-            imag = mixed_ref[(ROOT // 2 + k1) * ROOT : (ROOT // 2 + k1 + 1) * ROOT, :]
+            imag = mixed_ref[(ROOT // 2 + k1) * ROWS : (ROOT // 2 + k1 + 1) * ROWS, :]
             imag_turned = pltpu.roll(imag, HALF, 1)
         else:
             imag = jnp.zeros_like(real)
             imag_turned = imag
-        upper = jnp.concatenate(
-            [jnp.where(left, real, imag_turned), jnp.where(left, real_turned, imag)], axis=1
+        data = jnp.concatenate(
+            [
+                jnp.where(left, real, imag_turned),
+                jnp.where(left, real_turned, imag),
+                jnp.where(left, -imag, real_turned),
+                jnp.where(left, -imag_turned, real),
+            ],
+            axis=0,
         )
-        lower = jnp.concatenate(
-            [jnp.where(left, -imag, real_turned), jnp.where(left, -imag_turned, real)], axis=1
-        )
-        data = split_data(jnp.concatenate([upper, lower], axis=0), 0, "hlh")
-        result = jnp.dot(section_ref[k1], data, preferred_element_type=jnp.float32)
+        result = jnp.dot(section_ref[k1], split_data(data, 0, "hlh"), preferred_element_type=jnp.float32)
         count = KEPT // ROOT
-        for h in range(2):
-            start = (k1 // 8) * 16 + h * 8 + k1 % 8
-            out_ref[pl.ds(start, count, stride=LANES), :] = result[:count, h * LANES : (h + 1) * LANES]
+        store(k1, result[:count])
         if 0 < k1 < ROOT // 2:
-            other = ROOT - k1
-            mirrored = jnp.where(keep, result[count:], -result[count:])
-            for h in range(2):
-                start = (other // 8) * 16 + h * 8 + other % 8
-                out_ref[pl.ds(start, count, stride=LANES), :] = mirrored[:, h * LANES : (h + 1) * LANES]
-
-
-def x_transform(lines):
+            store(ROOT - k1, jnp.where(left, result[count:], -result[count:]))
+
+
+def x_first_kernel(place_ref, outer_ref, section_ref, lines_ref, *refs):
+    out_refs, mixed_ref, slots_ref = refs[:8], refs[8], refs[9]
+    zh, z = place_ref[0], place_ref[1]
+
+    def load_row(r):
+        parts = []
+        for source in range(4):
+            start = ((zh - source) & 3) * ROWS + r
+            parts.append(lines_ref[pl.ds(start, 16, stride=4 * ROWS), :])
+        return jnp.concatenate(parts, axis=0)
+
+    def store(k1, values):
+        for zh_out in range(4):
+            slot = (2 * zh_out + (k1 >> 4 & 1) - z) & 7
+            start = slot * SLOT + ((k1 >> 5) * 2 + (k1 >> 3 & 1)) * 8 + k1 % 8
+            slots_ref[pl.ds(start, 8, stride=32), :] = values[zh_out * 8 : zh_out * 8 + 8]
+
+    x_steps(outer_ref[...], section_ref, load_row, mixed_ref, store)
+    for slot in range(8):
+        out_refs[slot][...] = slots_ref[slot * SLOT : (slot + 1) * SLOT, :].reshape(32, 8, LANES)
+
+
+def x_second_kernel(place_ref, outer_ref, section_ref, *refs):
+    in_refs, out_ref, mixed_ref, lines_ref = refs[:4], refs[4], refs[5], refs[6]
+    zh, z = place_ref[0], place_ref[1]
+    for dz in range(4):
+        start = pl.multiple_of(((zh - dz) & 3) * (16 * ROWS), 16 * ROWS)
+        lines_ref[pl.ds(start, 16 * ROWS), :] = in_refs[dz][...].reshape(16 * ROWS, LANES)
+
+    def load_row(r):
+        return lines_ref[pl.ds(r, ROOT, stride=ROWS), :]
+
+    def store(k1, values):
+        for zh_out in range(4):
+            slot = (2 * zh_out + (k1 >> 4 & 1) - z) & 7
+            start = (((k1 >> 5) * 2 + (k1 >> 3 & 1)) * 8 + slot) * 8 + k1 % 8
+            out_ref[pl.ds(start, 8, stride=SLOT), :] = values[zh_out * 8 : zh_out * 8 + 8]
+
+    x_steps(outer_ref[...], section_ref, load_row, mixed_ref, store)
+
+
+def x_transform_first(lines, place):
     outer, sections = x_tables()
-    return pl.pallas_call(
-        x_kernel,
-        out_shape=jax.ShapeDtypeStruct((LENGTH, LANES), jnp.float32),
-        scratch_shapes=[pltpu.VMEM((LENGTH, LANES), jnp.float32)],
-        compiler_params=pltpu.CompilerParams(vmem_limit_bytes=40 << 20),
-        name="x_transform",
-    )(jnp.asarray(outer), jnp.asarray(sections), lines)
+    lines = lines.reshape(ROOT * ROWS, LANES)
+    scratch = [pltpu.VMEM((ROOT * ROWS, LANES), jnp.float32)] * 2
+    tables = [jnp.asarray(outer), jnp.asarray(sections)]
+    return call(x_first_kernel, "x_first", [floats(32, 8, LANES)] * 8, [place], *tables, lines, scratch=scratch)
+
+
+def x_transform_second(parts, place):
+    outer, sections = x_tables()
+    scratch = [pltpu.VMEM((ROOT * ROWS, LANES), jnp.float32)] * 2
+    tables = [jnp.asarray(outer), jnp.asarray(sections)]
+    out = call(x_second_kernel, "x_second", floats(8 * SLOT, LANES), [place], *tables, *parts, scratch=scratch)
+    return out.reshape(32, 8, 8, LANES)
 
 
 def add(p, q):
@@ -153,16 +253,20 @@
     return out
 
 
-def y_kernel(symbol_x_ref, table_ref, cosine_ref, sine_ref, symbol_ref, kz_ref, lines_ref, out_ref):
+def y_kernel(place_ref, symbol_x_ref, table_ref, cosine_ref, sine_ref, symbol_ref, kz_ref, first_ref, *refs):
+    second_refs, out_ref, lines_ref = refs[:8], refs[8], refs[9]
+    z = place_ref[1]
+    for dz in range(8):
+        start = pl.multiple_of(((z - dz) & 7) * SLOT, SLOT)
+        lines_ref[pl.ds(start, SLOT), :] = second_refs[dz][...].reshape(SLOT, LANES)
     table = table_ref[...]
     scale = -1.0 / math.sqrt(LENGTH * LENGTH)
     kz = kz_ref[...]
     for j in range(8):
-        rows = []
-        for h in range(2):
-            values = lines_ref[pl.ds(h * 8 + j, 256, stride=16), :]
-            rows.append(split_data(values.T, 1, "hlh"))
-        product = jnp.dot(jnp.concatenate(rows, axis=0), table, preferred_element_type=jnp.float32)
+        parts = [first_ref[pl.ds(((z - source) & 7) * 8 + j, 32, stride=64), :] for source in range(8)]
+        halves = [jnp.concatenate(parts, axis=0), lines_ref[pl.ds(j, 256, stride=8), :]]
+        rows = jnp.concatenate([split_data(half.T, 1, "hlh") for half in halves], axis=0)
+        product = jnp.dot(rows, table, preferred_element_type=jnp.float32)
         values = []
         for h in range(2):
             for m in range(8):
@@ -182,35 +286,54 @@
             out_ref[1, j, :, k * 256 : (k + 1) * 256] = imag * factor
 
 
-def y_transform(lines, symbol_x, kz_square):
+def y_transform(first, second, place, symbol_x, kz_square):
     table, cosine, sine_part, symbol = y_tables()
-    vmem = pl.BlockSpec(memory_space=pltpu.VMEM)
-    return pl.pallas_call(
+    return call(
         y_kernel,
-        out_shape=jax.ShapeDtypeStruct((2, 8, PLANES, LENGTH), jnp.float32),
-        in_specs=[pl.BlockSpec(memory_space=pltpu.SMEM)] + [vmem] * 6,
-        compiler_params=pltpu.CompilerParams(vmem_limit_bytes=40 << 20),
-        name="y_transform",
-    )(
-        symbol_x,
+        "y_transform",
+        floats(2, 8, PLANES, LENGTH),
+        [place, symbol_x],
         jnp.asarray(table),
         jnp.asarray(cosine),
         jnp.asarray(sine_part),
         jnp.asarray(symbol),
         jnp.broadcast_to(kz_square[:, None], (PLANES, 256)),
-        lines,
+        first.reshape(8 * SLOT, LANES),
+        *second,
+        scratch=[pltpu.VMEM((8 * SLOT, LANES), jnp.float32)],
     )
 
 
+def around(parts, axes):
+    count = len(parts)
+    return [
+        part if step == 0 else lax.ppermute(part, axes, [(i, (i + step) % count) for i in range(count)])
+        for step, part in enumerate(parts)
+    ]
+
+
+def across(whole, axes):
+    return lax.all_to_all(whole, axes, 0, 0, tiled=True)
+
+
 def body(density, kz_square):
-    gx = AXES[:3]
-    blocks = jnp.transpose(density.reshape(64, 64, LANES), (1, 0, 2))
-    lines = lax.all_to_all(blocks, gx, 0, 0, tiled=True)
-    spectrum = x_transform(lines.reshape(LENGTH, LANES))
-    lines = lax.all_to_all(spectrum.reshape(256, 16, LANES), AXES, 0, 0, tiled=True)
+    zh = lax.axis_index("zh")
+    z = zh * 2 + lax.axis_index("zl")
+    place = jnp.stack([zh, z]).astype(jnp.int32)
+    *first, second = pack(density, place)
+    first = around(first, "zh")
+    second = split(across(second, ("x", "y")))
+    first = across(join(first), ("x", "y"))
+    second = around(second, "zh")
+    first = x_transform_first(first, place)
+    first = around(first, ("zh", "zl"))
+    second = x_transform_second(second, place)
+    second = split(across(second, ("x", "y", "core")))
+    first = across(join(first), ("x", "y", "core"))
+    second = around(second, ("zh", "zl"))
     wave_x = (lax.axis_index(AXES) * 8 + jnp.arange(8, dtype=jnp.int32)).astype(jnp.float32)
     symbol_x = 4.0 * jnp.sin(wave_x * (math.pi / LENGTH)) ** 2
-    return y_transform(lines.reshape(LENGTH, LANES), symbol_x, kz_square)
+    return y_transform(first, second, place, symbol_x, kz_square)
 
 
 def solution(mesh):

time: 143 us -> 174 us (1.22)
  starting transfers between devices: 13.3 us -> 76.7 us
  blocking collectives: 62.1 us -> 0 us
  waiting for transfers between devices: 53.7 us -> 72.4 us
  Pallas kernels: 9.99 us -> 14.9 us
  local copies, waits for them, and re-layouts: 3.27 us -> 8.03 us
    ppermute x0 -> x20, waiting for transfers between devices: none -> 70.4 us  [around(): lax.ppermute(part, axes, [(i, (i + step) % count) for i in range(count)])]
    all_to_all x1 -> x0, blocking collectives: 62.1 us -> none  [body(): lines = lax.all_to_all(blocks, gx, 0, 0, tiled=True)]
    all_to_all x1 -> x4, waiting for transfers between devices: 53.7 us -> 2.01 us  [across(): return lax.all_to_all(whole, axes, 0, 0, tiled=True)]
    ppermute x0 -> x20, starting transfers between devices: none -> 47.1 us  [around(): lax.ppermute(part, axes, [(i, (i + step) % count) for i in range(count)])]
    all_to_all x1 -> x4, starting transfers between devices: 13.3 us -> 29.7 us  [across(): return lax.all_to_all(whole, axes, 0, 0, tiled=True)]
    unnamed x18 -> x28, local copies, waits for them, and re-layouts: 2.94 us -> 7.96 us
    pallas_call x2 -> x8, Pallas kernels: 9.99 us -> 14.9 us  [call(): pl.pallas_call(kernel, out_shape=out_shape, in_specs=[smem] * len(scalars...]
  transfers between devices with their start and end apart: 1 -> 24, of which waited for: 1 -> 14; matrix products, arithmetic and copies ran while one was open for 0% -> 0% of each run, Pallas kernels for 0% -> 5%
where the time goes in v1:
time: 174 us; the launch traced here: 172 us
  starting transfers between devices  76.7 us (44%)
  waiting for transfers between devices  72.4 us (42%)
  Pallas kernels  14.9 us (9%)
  local copies, waits for them, and re-layouts  8.03 us (5%)
    ppermute x20, waiting for transfers between devices, around(): lax.ppermute(part, axes, [(i, (i + step) % count) for i in range(count)])  70.4 us
    ppermute x20, starting transfers between devices, around(): lax.ppermute(part, axes, [(i, (i + step) % count) for i in range(count)])  47.1 us
    all_to_all x4, starting transfers between devices, across(): return lax.all_to_all(whole, axes, 0, 0, tiled=True)  29.7 us
    pallas_call x8, Pallas kernels, call(): pl.pallas_call(kernel, out_shape=out_shape, in_specs=[smem] * len(scalars...  14.9 us
    unnamed x28, local copies, waits for them, and re-layouts  7.96 us
  transfers between devices with their start and end apart: 24, of which 14 were waited for; matrix products, arithmetic and copies ran while one was open for 0% of the time, Pallas kernels for 5%

profile of v1, /device:TPU:1, one launch (start us, length us, event | category | flops | bytes accessed | tf_op | source)
XLA Modules:
  0.0 172.3 jit_solution(9591606277468815654)
XLA Ops:
  3.8 7.6 %all-to-all-start.2 = ((f32[16,4,32,128]{3,2,1,0:T(8,128)}), f32[16,4,32,128]{3,2,1,0:T(8,128)S(1)}, u32[]{:S(2)}, u32[]{:S(2)}) async-start(f32[16,4,32,128]{3,2,1,0:T(8,128)} %get-tuple-element.42), calls=%async_computation.2 | async-start | bytes 2097152 | tf_op jit(solution)/shard_map/all_to_all | solution.py:316
  11.4 3.1 %collective-permute-start = (f32[16,32,128]{2,1,0:T(8,128)S(1)}, f32[16,32,128]{2,1,0:T(8,128)S(1)}, u32[]{:S(2)}, u32[]{:S(2)}) collective-permute-start(f32[16,32,128]{2,1,0:T(8,128)S(1)} %get-tuple-element.31), channel_id=1, source_target_pairs={{0,64},{64,128},{128,192},{192,0},{1,65},{65,129},{129,193},{193,1... | collective-permute-start | bytes 786440 | tf_op jit(solution)/shard_map/ppermute | solution.py:310
  14.4 5.1 %collective-permute-start.1 = (f32[16,32,128]{2,1,0:T(8,128)S(1)}, f32[16,32,128]{2,1,0:T(8,128)S(1)}, u32[]{:S(2)}, u32[]{:S(2)}) collective-permute-start(f32[16,32,128]{2,1,0:T(8,128)S(1)} %get-tuple-element.32), channel_id=1, source_target_pairs={{0,128},{64,192},{128,0},{192,64},{1,129},{65,193},{129,1},{193,65... | collective-permute-start | bytes 786440 | tf_op jit(solution)/shard_map/ppermute | solution.py:310
  24.8 9.8 %collective-permute-done.1.refs_2_ = f32[16,32,128]{2,1,0:T(8,128)S(1)} collective-permute-done((f32[16,32,128]{2,1,0:T(8,128)S(1)}, f32[16,32,128]{2,1,0:T(8,128)S(1)}, u32[]{:S(2)}, u32[]{:S(2)}) %collective-permute-start.1) | collective-permute-done | bytes 262176 | tf_op jit(solution)/shard_map/ppermute | solution.py:310
  34.6 9.2 %collective-permute-done.2.refs_3_ = f32[16,32,128]{2,1,0:T(8,128)S(1)} collective-permute-done((f32[16,32,128]{2,1,0:T(8,128)S(1)}, f32[16,32,128]{2,1,0:T(8,128)S(1)}, u32[]{:S(2)}, u32[]{:S(2)}) %collective-permute-start.2) | collective-permute-done | bytes 262176 | tf_op jit(solution)/shard_map/ppermute | solution.py:310
  45.9 6.4 %all-to-all-start = ((f32[16,4,32,128]{3,2,1,0:T(8,128)}), f32[16,4,32,128]{3,2,1,0:T(8,128)S(1)}, u32[]{:S(2)}, u32[]{:S(2)}) async-start(f32[16,4,32,128]{3,2,1,0:T(8,128)} %copy-done.3), calls=%async_computation | async-start | bytes 2097152 | tf_op jit(solution)/shard_map/all_to_all | solution.py:316
  54.6 4.2 %collective-permute-start.11 = (f32[16,32,128]{2,1,0:T(8,128)S(1)}, f32[16,32,128]{2,1,0:T(8,128)S(1)}, u32[]{:S(2)}, u32[]{:S(2)}) collective-permute-start(f32[16,32,128]{2,1,0:T(8,128)S(1)} %get-tuple-element.45), channel_id=1, source_target_pairs={{0,128},{64,192},{128,0},{192,64},{1,129},{65,193},{129,1},{193,65... | collective-permute-start | bytes 786440 | tf_op jit(solution)/shard_map/ppermute | solution.py:310
  60.8 4.8 %collective-permute-done.10.refs_1_ = f32[16,32,128]{2,1,0:T(8,128)S(1)} collective-permute-done((f32[16,32,128]{2,1,0:T(8,128)S(1)}, f32[16,32,128]{2,1,0:T(8,128)S(1)}, u32[]{:S(2)}, u32[]{:S(2)}) %collective-permute-start.10) | collective-permute-done | bytes 262176 | tf_op jit(solution)/shard_map/ppermute | solution.py:310
  65.6 12.9 %collective-permute-done.11.refs_2_ = f32[16,32,128]{2,1,0:T(8,128)S(1)} collective-permute-done((f32[16,32,128]{2,1,0:T(8,128)S(1)}, f32[16,32,128]{2,1,0:T(8,128)S(1)}, u32[]{:S(2)}, u32[]{:S(2)}) %collective-permute-start.11) | collective-permute-done | bytes 262176 | tf_op jit(solution)/shard_map/ppermute | solution.py:310
  83.5 7.8 %all-to-all-start.3 = ((f32[32,8,8,128]{3,2,1,0:T(8,128)}), f32[32,8,8,128]{3,2,1,0:T(8,128)S(1)}, u32[]{:S(2)}, u32[]{:S(2)}) async-start(f32[32,8,8,128]{3,2,1,0:T(8,128)} %bitcast.7), calls=%async_computation.3 | async-start | bytes 2097152 | tf_op jit(solution)/shard_map/all_to_all | solution.py:316
  92.5 3.3 %x_first.1 = (f32[32,8,128]{2,1,0:T(8,128)S(1)}, f32[32,8,128]{2,1,0:T(8,128)S(1)}, f32[32,8,128]{2,1,0:T(8,128)S(1)}, f32[32,8,128]{2,1,0:T(8,128)S(1)}, f32[32...) custom-call(s32[2]{0:T(128)S(1)} %pad_add_fusion.place_ref, ...), custom_call_target="tpu_custom_call" | custom-call | tf_op jit(solution)/shard_map/x_first/pallas_call | solution.py:103
  96.1 4.4 %collective-permute-start.5 = (f32[32,8,128]{2,1,0:T(8,128)S(1)}, f32[32,8,128]{2,1,0:T(8,128)S(1)}, u32[]{:S(2)}, u32[]{:S(2)}) collective-permute-start(f32[32,8,128]{2,1,0:T(8,128)S(1)} %get-tuple-element.37), channel_id=1, source_target_pairs={{0,66},{2,128},{64,130},{66,192},{128,194},{130,0},{192,2},{194,64... | collective-permute-start | bytes 393224 | tf_op jit(solution)/shard_map/ppermute | solution.py:310
  101.5 3.7 %collective-permute-start.7 = (f32[32,8,128]{2,1,0:T(8,128)S(1)}, f32[32,8,128]{2,1,0:T(8,128)S(1)}, u32[]{:S(2)}, u32[]{:S(2)}) collective-permute-start(f32[32,8,128]{2,1,0:T(8,128)S(1)} %get-tuple-element.39), channel_id=1, source_target_pairs={{0,130},{2,192},{64,194},{66,0},{128,2},{130,64},{192,66},{194,128... | collective-permute-start | bytes 393224 | tf_op jit(solution)/shard_map/ppermute | solution.py:310
  107.1 4.0 %collective-permute-start.9 = (f32[32,8,128]{2,1,0:T(8,128)S(1)}, f32[32,8,128]{2,1,0:T(8,128)S(1)}, u32[]{:S(2)}, u32[]{:S(2)}) collective-permute-start(f32[32,8,128]{2,1,0:T(8,128)S(1)} %get-tuple-element.41), channel_id=1, source_target_pairs={{0,194},{2,0},{64,2},{66,64},{128,66},{130,128},{192,130},{194,192... | collective-permute-start | bytes 393224 | tf_op jit(solution)/shard_map/ppermute | solution.py:310
  111.0 6.0 %collective-permute-done.5.refs_3_ = f32[32,8,128]{2,1,0:T(8,128)S(1)} collective-permute-done((f32[32,8,128]{2,1,0:T(8,128)S(1)}, f32[32,8,128]{2,1,0:T(8,128)S(1)}, u32[]{:S(2)}, u32[]{:S(2)}) %collective-permute-start.5) | collective-permute-done | bytes 131104 | tf_op jit(solution)/shard_map/ppermute | solution.py:310
  118.6 6.7 %collective-permute-done.8.refs_6_ = f32[32,8,128]{2,1,0:T(8,128)S(1)} collective-permute-done((f32[32,8,128]{2,1,0:T(8,128)S(1)}, f32[32,8,128]{2,1,0:T(8,128)S(1)}, u32[]{:S(2)}, u32[]{:S(2)}) %collective-permute-start.8) | collective-permute-done | bytes 131104 | tf_op jit(solution)/shard_map/ppermute | solution.py:310
  126.5 7.9 %all-to-all-start.1 = ((f32[32,8,8,128]{3,2,1,0:T(8,128)}), f32[32,8,8,128]{3,2,1,0:T(8,128)S(1)}, u32[]{:S(2)}, u32[]{:S(2)}) async-start(f32[32,8,8,128]{3,2,1,0:T(8,128)} %join.3), calls=%async_computation.1 | async-start | bytes 2097152 | tf_op jit(solution)/shard_map/all_to_all | solution.py:316
  135.2 3.0 %collective-permute-start.13 = (f32[32,8,128]{2,1,0:T(8,128)S(1)}, f32[32,8,128]{2,1,0:T(8,128)S(1)}, u32[]{:S(2)}, u32[]{:S(2)}) collective-permute-start(f32[32,8,128]{2,1,0:T(8,128)S(1)} %get-tuple-element.48), channel_id=1, source_target_pairs={{0,2},{2,64},{64,66},{66,128},{128,130},{130,192},{192,194},{194,0... | collective-permute-start | bytes 393224 | tf_op jit(solution)/shard_map/ppermute | solution.py:310
  140.8 3.0 %collective-permute-start.16 = (f32[32,8,128]{2,1,0:T(8,128)}, f32[32,8,128]{2,1,0:T(8,128)S(1)}, u32[]{:S(2)}, u32[]{:S(2)}) collective-permute-start(f32[32,8,128]{2,1,0:T(8,128)} %get-tuple-element.51), channel_id=1, source_target_pairs={{0,128},{2,130},{64,192},{66,194},{128,0},{130,2},{192,64},{194,66... | collective-permute-start | bytes 393224 | tf_op jit(solution)/shard_map/ppermute | solution.py:310
  145.2 3.3 %collective-permute-start.18 = (f32[32,8,128]{2,1,0:T(8,128)S(1)}, f32[32,8,128]{2,1,0:T(8,128)S(1)}, u32[]{:S(2)}, u32[]{:S(2)}) collective-permute-start(f32[32,8,128]{2,1,0:T(8,128)S(1)} %get-tuple-element.53), channel_id=1, source_target_pairs={{0,192},{2,194},{64,0},{66,2},{128,64},{130,66},{192,128},{194,130... | collective-permute-start | bytes 393224 | tf_op jit(solution)/shard_map/ppermute | solution.py:310
  151.3 5.2 %collective-permute-done.15.refs_3_ = f32[32,8,128]{2,1,0:T(8,128)S(1)} collective-permute-done((f32[32,8,128]{2,1,0:T(8,128)}, f32[32,8,128]{2,1,0:T(8,128)S(1)}, u32[]{:S(2)}, u32[]{:S(2)}) %collective-permute-start.15) | collective-permute-done | bytes 131104 | tf_op jit(solution)/shard_map/ppermute | solution.py:310
  156.5 3.7 %collective-permute-done.16.refs_4_ = f32[32,8,128]{2,1,0:T(8,128)S(1)} collective-permute-done((f32[32,8,128]{2,1,0:T(8,128)}, f32[32,8,128]{2,1,0:T(8,128)S(1)}, u32[]{:S(2)}, u32[]{:S(2)}) %collective-permute-start.16) | collective-permute-done | bytes 131104 | tf_op jit(solution)/shard_map/ppermute | solution.py:310
  161.1 6.0 %collective-permute-done.18.refs_6_ = f32[32,8,128]{2,1,0:T(8,128)S(1)} collective-permute-done((f32[32,8,128]{2,1,0:T(8,128)S(1)}, f32[32,8,128]{2,1,0:T(8,128)S(1)}, u32[]{:S(2)}, u32[]{:S(2)}) %collective-permute-start.18) | collective-permute-done | bytes 131104 | tf_op jit(solution)/shard_map/ppermute | solution.py:310
  167.8 4.5 %y_transform.1 = f32[2,8,8,4096]{3,2,1,0:T(8,128)} custom-call(s32[2]{0:T(128)S(1)} %pad_add_fusion.place_ref, f32[8]{0:T(128)S(1)} %multiply_multiply_fusion.symbol_x_ref, bf16[768,512]{1,0:T(8,128)(2,1)S(1)} %copy-done.8, f32[16,256]{1,0:T(8,128)S(1)} %copy-done.12, f32[16,256]{1,0:T(8,128)S(1)} %copy-done.11, f32[16,256]{1,0:T(8,128)S(1)} %copy-done.10, ...), custom_call_target="tpu_custom_call" | custom-call | tf_op jit(solution)/shard_map/y_transform/pallas_call | solution.py:103
  (63 shorter events, 36.6 us)
Async XLA Ops:
  3.8 41.1 %all-to-all-start.2 = ((f32[16,4,32,128]{3,2,1,0:T(8,128)}), f32[16,4,32,128]{3,2,1,0:T(8,128)S(1)}, u32[]{:S(2)}, u32[]{:S(2)}) async-start(f32[16,4,32,128]{3,2,1,0:T(8,128)} %get-tuple-element.42), calls=%async_computation.2 | async-start | bytes 2097152 | tf_op jit(solution)/shard_map/all_to_all | solution.py:316
  11.4 13.4 %collective-permute-start = (f32[16,32,128]{2,1,0:T(8,128)S(1)}, f32[16,32,128]{2,1,0:T(8,128)S(1)}, u32[]{:S(2)}, u32[]{:S(2)}) collective-permute-start(f32[16,32,128]{2,1,0:T(8,128)S(1)} %get-tuple-element.31), channel_id=1, source_target_pairs={{0,64},{64,128},{128,192},{192,0},{1,65},{65,129},{129,193},{193,1... | collective-permute-start | bytes 786440 | tf_op jit(solution)/shard_map/ppermute | solution.py:310
  14.4 20.1 %collective-permute-start.1 = (f32[16,32,128]{2,1,0:T(8,128)S(1)}, f32[16,32,128]{2,1,0:T(8,128)S(1)}, u32[]{:S(2)}, u32[]{:S(2)}) collective-permute-start(f32[16,32,128]{2,1,0:T(8,128)S(1)} %get-tuple-element.32), channel_id=1, source_target_pairs={{0,128},{64,192},{128,0},{192,64},{1,129},{65,193},{129,1},{193,65... | collective-permute-start | bytes 786440 | tf_op jit(solution)/shard_map/ppermute | solution.py:310
  19.5 24.3 %collective-permute-start.2 = (f32[16,32,128]{2,1,0:T(8,128)S(1)}, f32[16,32,128]{2,1,0:T(8,128)S(1)}, u32[]{:S(2)}, u32[]{:S(2)}) collective-permute-start(f32[16,32,128]{2,1,0:T(8,128)S(1)} %get-tuple-element.33), channel_id=1, source_target_pairs={{0,192},{64,0},{128,64},{192,128},{1,193},{65,1},{129,65},{193,129... | collective-permute-start | bytes 786440 | tf_op jit(solution)/shard_map/ppermute | solution.py:310
  45.9 36.6 %all-to-all-start = ((f32[16,4,32,128]{3,2,1,0:T(8,128)}), f32[16,4,32,128]{3,2,1,0:T(8,128)S(1)}, u32[]{:S(2)}, u32[]{:S(2)}) async-start(f32[16,4,32,128]{3,2,1,0:T(8,128)} %copy-done.3), calls=%async_computation | async-start | bytes 2097152 | tf_op jit(solution)/shard_map/all_to_all | solution.py:316
  53.6 12.0 %collective-permute-start.10 = (f32[16,32,128]{2,1,0:T(8,128)S(1)}, f32[16,32,128]{2,1,0:T(8,128)S(1)}, u32[]{:S(2)}, u32[]{:S(2)}) collective-permute-start(f32[16,32,128]{2,1,0:T(8,128)S(1)} %get-tuple-element.44), channel_id=1, source_target_pairs={{0,64},{64,128},{128,192},{192,0},{1,65},{65,129},{129,193},{193,1... | collective-permute-start | bytes 786440 | tf_op jit(solution)/shard_map/ppermute | solution.py:310
  54.6 24.0 %collective-permute-start.11 = (f32[16,32,128]{2,1,0:T(8,128)S(1)}, f32[16,32,128]{2,1,0:T(8,128)S(1)}, u32[]{:S(2)}, u32[]{:S(2)}) collective-permute-start(f32[16,32,128]{2,1,0:T(8,128)S(1)} %get-tuple-element.45), channel_id=1, source_target_pairs={{0,128},{64,192},{128,0},{192,64},{1,129},{65,193},{129,1},{193,65... | collective-permute-start | bytes 786440 | tf_op jit(solution)/shard_map/ppermute | solution.py:310
  58.8 19.8 %collective-permute-start.12 = (f32[16,32,128]{2,1,0:T(8,128)S(1)}, f32[16,32,128]{2,1,0:T(8,128)S(1)}, u32[]{:S(2)}, u32[]{:S(2)}) collective-permute-start(f32[16,32,128]{2,1,0:T(8,128)S(1)} %get-tuple-element.46), channel_id=1, source_target_pairs={{0,192},{64,0},{128,64},{192,128},{1,193},{65,1},{129,65},{193,129... | collective-permute-start | bytes 786440 | tf_op jit(solution)/shard_map/ppermute | solution.py:310
  83.5 43.0 %all-to-all-start.3 = ((f32[32,8,8,128]{3,2,1,0:T(8,128)}), f32[32,8,8,128]{3,2,1,0:T(8,128)S(1)}, u32[]{:S(2)}, u32[]{:S(2)}) async-start(f32[32,8,8,128]{3,2,1,0:T(8,128)} %bitcast.7), calls=%async_computation.3 | async-start | bytes 2097152 | tf_op jit(solution)/shard_map/all_to_all | solution.py:316
  95.8 9.4 %collective-permute-start.3 = (f32[32,8,128]{2,1,0:T(8,128)S(1)}, f32[32,8,128]{2,1,0:T(8,128)S(1)}, u32[]{:S(2)}, u32[]{:S(2)}) collective-permute-start(f32[32,8,128]{2,1,0:T(8,128)S(1)} %get-tuple-element.35), channel_id=1, source_target_pairs={{0,2},{2,64},{64,66},{66,128},{128,130},{130,192},{192,194},{194,0... | collective-permute-start | bytes 393224 | tf_op jit(solution)/shard_map/ppermute | solution.py:310
  95.8 11.2 %collective-permute-start.4 = (f32[32,8,128]{2,1,0:T(8,128)S(1)}, f32[32,8,128]{2,1,0:T(8,128)S(1)}, u32[]{:S(2)}, u32[]{:S(2)}) collective-permute-start(f32[32,8,128]{2,1,0:T(8,128)S(1)} %get-tuple-element.36), channel_id=1, source_target_pairs={{0,64},{2,66},{64,128},{66,130},{128,192},{130,194},{192,0},{194,2... | collective-permute-start | bytes 393224 | tf_op jit(solution)/shard_map/ppermute | solution.py:310
  96.1 20.9 %collective-permute-start.5 = (f32[32,8,128]{2,1,0:T(8,128)S(1)}, f32[32,8,128]{2,1,0:T(8,128)S(1)}, u32[]{:S(2)}, u32[]{:S(2)}) collective-permute-start(f32[32,8,128]{2,1,0:T(8,128)S(1)} %get-tuple-element.37), channel_id=1, source_target_pairs={{0,66},{2,128},{64,130},{66,192},{128,194},{130,0},{192,2},{194,64... | collective-permute-start | bytes 393224 | tf_op jit(solution)/shard_map/ppermute | solution.py:310
  100.5 18.1 %collective-permute-start.6 = (f32[32,8,128]{2,1,0:T(8,128)S(1)}, f32[32,8,128]{2,1,0:T(8,128)S(1)}, u32[]{:S(2)}, u32[]{:S(2)}) collective-permute-start(f32[32,8,128]{2,1,0:T(8,128)S(1)} %get-tuple-element.38), channel_id=1, source_target_pairs={{0,128},{2,130},{64,192},{66,194},{128,0},{130,2},{192,64},{194,66... | collective-permute-start | bytes 393224 | tf_op jit(solution)/shard_map/ppermute | solution.py:310
  101.5 17.1 %collective-permute-start.7 = (f32[32,8,128]{2,1,0:T(8,128)S(1)}, f32[32,8,128]{2,1,0:T(8,128)S(1)}, u32[]{:S(2)}, u32[]{:S(2)}) collective-permute-start(f32[32,8,128]{2,1,0:T(8,128)S(1)} %get-tuple-element.39), channel_id=1, source_target_pairs={{0,130},{2,192},{64,194},{66,0},{128,2},{130,64},{192,66},{194,128... | collective-permute-start | bytes 393224 | tf_op jit(solution)/shard_map/ppermute | solution.py:310
  105.2 20.2 %collective-permute-start.8 = (f32[32,8,128]{2,1,0:T(8,128)S(1)}, f32[32,8,128]{2,1,0:T(8,128)S(1)}, u32[]{:S(2)}, u32[]{:S(2)}) collective-permute-start(f32[32,8,128]{2,1,0:T(8,128)S(1)} %get-tuple-element.40), channel_id=1, source_target_pairs={{0,192},{2,194},{64,0},{66,2},{128,64},{130,66},{192,128},{194,130... | collective-permute-start | bytes 393224 | tf_op jit(solution)/shard_map/ppermute | solution.py:310
  107.1 18.3 %collective-permute-start.9 = (f32[32,8,128]{2,1,0:T(8,128)S(1)}, f32[32,8,128]{2,1,0:T(8,128)S(1)}, u32[]{:S(2)}, u32[]{:S(2)}) collective-permute-start(f32[32,8,128]{2,1,0:T(8,128)S(1)} %get-tuple-element.41), channel_id=1, source_target_pairs={{0,194},{2,0},{64,2},{66,64},{128,66},{130,128},{192,130},{194,192... | collective-permute-start | bytes 393224 | tf_op jit(solution)/shard_map/ppermute | solution.py:310
  126.5 24.8 %all-to-all-start.1 = ((f32[32,8,8,128]{3,2,1,0:T(8,128)}), f32[32,8,8,128]{3,2,1,0:T(8,128)S(1)}, u32[]{:S(2)}, u32[]{:S(2)}) async-start(f32[32,8,8,128]{3,2,1,0:T(8,128)} %join.3), calls=%async_computation.1 | async-start | bytes 2097152 | tf_op jit(solution)/shard_map/all_to_all | solution.py:316
  135.2 10.0 %collective-permute-start.13 = (f32[32,8,128]{2,1,0:T(8,128)S(1)}, f32[32,8,128]{2,1,0:T(8,128)S(1)}, u32[]{:S(2)}, u32[]{:S(2)}) collective-permute-start(f32[32,8,128]{2,1,0:T(8,128)S(1)} %get-tuple-element.48), channel_id=1, source_target_pairs={{0,2},{2,64},{64,66},{66,128},{128,130},{130,192},{192,194},{194,0... | collective-permute-start | bytes 393224 | tf_op jit(solution)/shard_map/ppermute | solution.py:310
  138.1 10.4 %collective-permute-start.14 = (f32[32,8,128]{2,1,0:T(8,128)S(1)}, f32[32,8,128]{2,1,0:T(8,128)S(1)}, u32[]{:S(2)}, u32[]{:S(2)}) collective-permute-start(f32[32,8,128]{2,1,0:T(8,128)S(1)} %get-tuple-element.49), channel_id=1, source_target_pairs={{0,64},{2,66},{64,128},{66,130},{128,192},{130,194},{192,0},{194,2... | collective-permute-start | bytes 393224 | tf_op jit(solution)/shard_map/ppermute | solution.py:310
  139.8 16.7 %collective-permute-start.15 = (f32[32,8,128]{2,1,0:T(8,128)}, f32[32,8,128]{2,1,0:T(8,128)S(1)}, u32[]{:S(2)}, u32[]{:S(2)}) collective-permute-start(f32[32,8,128]{2,1,0:T(8,128)} %get-tuple-element.50), channel_id=1, source_target_pairs={{0,66},{2,128},{64,130},{66,192},{128,194},{130,0},{192,2},{194,64... | collective-permute-start | bytes 393224 | tf_op jit(solution)/shard_map/ppermute | solution.py:310
  140.8 19.4 %collective-permute-start.16 = (f32[32,8,128]{2,1,0:T(8,128)}, f32[32,8,128]{2,1,0:T(8,128)S(1)}, u32[]{:S(2)}, u32[]{:S(2)}) collective-permute-start(f32[32,8,128]{2,1,0:T(8,128)} %get-tuple-element.51), channel_id=1, source_target_pairs={{0,128},{2,130},{64,192},{66,194},{128,0},{130,2},{192,64},{194,66... | collective-permute-start | bytes 393224 | tf_op jit(solution)/shard_map/ppermute | solution.py:310
  143.8 17.3 %collective-permute-start.17 = (f32[32,8,128]{2,1,0:T(8,128)S(1)}, f32[32,8,128]{2,1,0:T(8,128)S(1)}, u32[]{:S(2)}, u32[]{:S(2)}) collective-permute-start(f32[32,8,128]{2,1,0:T(8,128)S(1)} %get-tuple-element.52), channel_id=1, source_target_pairs={{0,130},{2,192},{64,194},{66,0},{128,2},{130,64},{192,66},{194,128... | collective-permute-start | bytes 393224 | tf_op jit(solution)/shard_map/ppermute | solution.py:310
  145.2 21.9 %collective-permute-start.18 = (f32[32,8,128]{2,1,0:T(8,128)S(1)}, f32[32,8,128]{2,1,0:T(8,128)S(1)}, u32[]{:S(2)}, u32[]{:S(2)}) collective-permute-start(f32[32,8,128]{2,1,0:T(8,128)S(1)} %get-tuple-element.53), channel_id=1, source_target_pairs={{0,192},{2,194},{64,0},{66,2},{128,64},{130,66},{192,128},{194,130... | collective-permute-start | bytes 393224 | tf_op jit(solution)/shard_map/ppermute | solution.py:310
  148.5 19.2 %collective-permute-start.19 = (f32[32,8,128]{2,1,0:T(8,128)S(1)}, f32[32,8,128]{2,1,0:T(8,128)S(1)}, u32[]{:S(2)}, u32[]{:S(2)}) collective-permute-start(f32[32,8,128]{2,1,0:T(8,128)S(1)} %get-tuple-element.54), channel_id=1, source_target_pairs={{0,194},{2,0},{64,2},{66,64},{128,66},{130,128},{192,130},{194,192... | collective-permute-start | bytes 393224 | tf_op jit(solution)/shard_map/ppermute | solution.py:310
  (14 other events, 282.1 us)

commit v2 on v0

v2 whole, which is shorter than its diff:
```python
import functools
import math

import jax
import jax.numpy as jnp
import ml_dtypes
import numpy as np
from jax import lax
from jax.experimental import pallas as pl
from jax.experimental.pallas import tpu as pltpu
from jax.sharding import Mesh
from jax.sharding import PartitionSpec as P

LENGTH = 4096
KEPT = 2048
ROOT = 64
LANES = 128
PITCH = 72
PLANES = 8
AXES = ("zh", "x", "y", "zl", "core")


def split_table(table, axis, order):
    high = table.astype(ml_dtypes.bfloat16)
    low = (table - high.astype(np.float64)).astype(ml_dtypes.bfloat16)
    parts = {"h": high, "l": low}
    return np.concatenate([parts[name] for name in order], axis=axis)


def split_data(values, axis, order):
    high = values.astype(jnp.bfloat16)
    low = (values - high.astype(jnp.float32)).astype(jnp.bfloat16)
    parts = {"h": high, "l": low}
    return jnp.concatenate([parts[name] for name in order], axis=axis)


@functools.cache
def x_tables():
    a = np.arange(ROOT)
    first = 2.0 * np.pi * np.outer(np.arange(ROOT // 2 + 1), a) / ROOT
    outer = np.concatenate([np.cos(first), -np.sin(first[1 : ROOT // 2])], axis=0)
    sections = []
    k2 = np.arange(KEPT // ROOT)
    for k1 in range(ROOT // 2 + 1):
        rows = []
        for k in (k1, (ROOT - k1) % ROOT):
            angle = 2.0 * np.pi * np.outer(k + ROOT * k2, a) / LENGTH
            rows += [np.cos(angle), np.sin(angle)]
        sections.append(np.concatenate(rows, axis=0))
    return split_table(outer, 1, "hhl"), split_table(np.stack(sections), 2, "hhl")


@functools.cache
def y_tables():
    source = np.arange(256)
    place = (source % 4) * 64 + source // 4
    angle = 2.0 * np.pi * np.outer(place, np.arange(256)) / 256
    table = np.concatenate([np.cos(angle), -np.sin(angle)], axis=1)
    turn = 2.0 * np.pi * np.outer(np.arange(16), np.arange(256)) / LENGTH
    wave = np.arange(LENGTH).reshape(16, 256)
    symbol = 4.0 * np.sin(np.pi * wave / LENGTH) ** 2
    return (
        split_table(table, 0, "hhl"),
        np.cos(turn).astype(np.float32),
        (-np.sin(turn)).astype(np.float32),
        symbol.astype(np.float32),
    )


def x_kernel(outer_ref, section_ref, lines_ref, out_ref, mixed_ref):
    outer = outer_ref[...]
    for b in range(0, ROOT, 2):
        pair = jnp.concatenate(
            [lines_ref[pl.ds(b + i, ROOT, stride=ROOT), :] for i in range(2)], axis=1
        )
        mixed = jnp.dot(outer, split_data(pair, 0, "hlh"), preferred_element_type=jnp.float32)
        for i in range(2):
            mixed_ref[pl.ds(b + i, ROOT, stride=PITCH), :] = mixed[:, i * LANES : (i + 1) * LANES]
    count = KEPT // ROOT

    def store(k1, part, values):
        start = (k1 // 8) * 16 + part * 8 + k1 % 8
        out_ref[pl.ds(start, count, stride=LANES), :] = values

    for k1 in range(ROOT // 2 + 1):
        real = mixed_ref[k1 * PITCH : k1 * PITCH + ROOT, :]
        if 0 < k1 < ROOT // 2:
            at = (ROOT // 2 + k1) * PITCH
            values = jnp.concatenate([real, mixed_ref[at : at + ROOT, :]], axis=1)
            result = jnp.dot(section_ref[k1], split_data(values, 0, "hlh"), preferred_element_type=jnp.float32)
            cosine, sine_part = result[:count], result[count : 2 * count]
            store(k1, 0, cosine[:, :LANES] + sine_part[:, LANES:])
            store(k1, 1, cosine[:, LANES:] - sine_part[:, :LANES])
            cosine, sine_part = result[2 * count : 3 * count], result[3 * count :]
            store(ROOT - k1, 0, cosine[:, :LANES] - sine_part[:, LANES:])
            store(ROOT - k1, 1, -cosine[:, LANES:] - sine_part[:, :LANES])
        else:
            section = section_ref[k1, : 2 * count, :]
            result = jnp.dot(section, split_data(real, 0, "hlh"), preferred_element_type=jnp.float32)
            store(k1, 0, result[:count])
            store(k1, 1, -result[count:])


def x_transform(lines):
    outer, sections = x_tables()
    return pl.pallas_call(
        x_kernel,
        out_shape=jax.ShapeDtypeStruct((LENGTH, LANES), jnp.float32),
        scratch_shapes=[pltpu.VMEM((ROOT * PITCH, LANES), jnp.float32)],
        compiler_params=pltpu.CompilerParams(vmem_limit_bytes=40 << 20),
        name="x_transform",
    )(jnp.asarray(outer), jnp.asarray(sections), lines)


def add(p, q):
    return (p[0] + q[0], p[1] + q[1])


def sub(p, q):
    return (p[0] - q[0], p[1] - q[1])


def turn_back(p):
    return (p[1], -p[0])


def times(p, angle):
    cosine, sine_part = math.cos(angle), math.sin(angle)
    return (p[0] * cosine - p[1] * sine_part, p[1] * cosine + p[0] * sine_part)


def four(p, q, r, s):
    even, odd = add(p, r), add(q, s)
    even_minus, odd_minus = sub(p, r), turn_back(sub(q, s))
    return add(even, odd), add(even_minus, odd_minus), sub(even, odd), sub(even_minus, odd_minus)


def sixteen(values):
    columns = []
    for n in range(4):
        column = four(*[values[4 * m + n] for m in range(4)])
        columns.append([times(v, -2.0 * math.pi * n * k / 16) if n * k else v for k, v in enumerate(column)])
    out = [None] * 16
    for k in range(4):
        for l, v in enumerate(four(*[columns[n][k] for n in range(4)])):
            out[k + 4 * l] = v
    return out


def y_kernel(place_ref, symbol_x_ref, kz_ref, table_ref, cosine_ref, sine_ref, symbol_ref, lines_ref, out_ref, done_ref, sent):
    table = table_ref[...]
    scale = -1.0 / math.sqrt(LENGTH * LENGTH)
    row = lax.broadcasted_iota(jnp.int32, (PLANES, 256), 0)
    kz = jnp.zeros((PLANES, 256), jnp.float32)
    for p in range(PLANES):
        kz = jnp.where(row == p, kz_ref[p], kz)
    copies = []
    for j in range(8):
        rows = []
        for part in range(2):
            values = lines_ref[pl.ds(part * 8 + j, 256, stride=16), :]
            rows.append(split_data(values.T, 1, "hlh"))
        product = jnp.dot(jnp.concatenate(rows, axis=0), table, preferred_element_type=jnp.float32)
        values = []
        for n in range(16):
            first = product[n * 8 : n * 8 + 8]
            second = product[LANES + n * 8 : LANES + n * 8 + 8]
            real = first[:, :256] - second[:, 256:]
            imag = first[:, 256:] + second[:, :256]
            if n:
                cosine, sine_part = cosine_ref[n : n + 1, :], sine_ref[n : n + 1, :]
                real, imag = real * cosine - imag * sine_part, imag * cosine + real * sine_part
            values.append((real, imag))
        shift = kz + symbol_x_ref[place_ref[0] * 8 + j]
        for k, (real, imag) in enumerate(sixteen(values)):
            factor = scale / (shift + symbol_ref[k : k + 1, :])
            done_ref[j, 0, :, k * 256 : (k + 1) * 256] = real * factor
            done_ref[j, 1, :, k * 256 : (k + 1) * 256] = imag * factor
        copies.append(pltpu.make_async_copy(done_ref.at[j], out_ref.at[:, j], sent.at[j]))
        copies[-1].start()
    for copy in copies:
        copy.wait()


def y_transform(lines, place, kz_square):
    table, cosine, sine_part, symbol = y_tables()
    symbol_x = (4.0 * np.sin(np.pi * np.arange(KEPT) / LENGTH) ** 2).astype(np.float32)
    vmem = pl.BlockSpec(memory_space=pltpu.VMEM)
    smem = pl.BlockSpec(memory_space=pltpu.SMEM)
    return pl.pallas_call(
        y_kernel,
        out_shape=jax.ShapeDtypeStruct((2, 8, PLANES, LENGTH), jnp.float32),
        in_specs=[smem] * 3 + [vmem] * 5,
        out_specs=pl.BlockSpec(memory_space=pl.ANY),
        scratch_shapes=[
            pltpu.VMEM((8, 2, PLANES, LENGTH), jnp.float32),
            pltpu.SemaphoreType.DMA((8,)),
        ],
        compiler_params=pltpu.CompilerParams(vmem_limit_bytes=40 << 20),
        name="y_transform",
    )(
        place,
        jnp.asarray(symbol_x),
        kz_square,
        jnp.asarray(table),
        jnp.asarray(cosine),
        jnp.asarray(sine_part),
        jnp.asarray(symbol),
        lines,
    )


def body(density, kz_square):
    place = jnp.stack([lax.axis_index(AXES)]).astype(jnp.int32)
    blocks = jnp.transpose(density.reshape(ROOT, ROOT, LANES), (1, 0, 2))
    lines = lax.all_to_all(blocks, AXES[:3], 0, 0, tiled=True)
    spectrum = x_transform(lines.reshape(LENGTH, LANES))
    lines = lax.all_to_all(spectrum.reshape(256, 16, LANES), AXES, 0, 0, tiled=True)
    return y_transform(lines.reshape(LENGTH, LANES), place, kz_square)


def solution(mesh):
    fine = Mesh(mesh.devices.reshape(4, 4, 4, 2, 2), AXES)
    in_specs = (P(AXES[:3], AXES[3:]), P())
    out_specs = P(None, AXES, None, None)
    return jax.shard_map(body, mesh=fine, in_specs=in_specs, out_specs=out_specs, check_vma=False)
```

time: 143 us -> 141 us (0.986)
    unnamed x18 -> x20, local copies, waits for them, and re-layouts: 2.94 us -> 2.95 us
where the time goes in v2:
time: 141 us
  blocking collectives  62.1 us (44%)
  waiting for transfers between devices  53.8 us (38%)
  starting transfers between devices  13.3 us (9%)
  Pallas kernels  8.57 us (6%)
  local copies, waits for them, and re-layouts  3.21 us (2%)
    all_to_all x1, blocking collectives, body(): lines = lax.all_to_all(blocks, AXES[:3], 0, 0, tiled=True)  62.1 us
    all_to_all x1, waiting for transfers between devices, body(): lax.all_to_all(spectrum.reshape(256, 16, LANES), AXES, 0, 0, tiled=True)  53.8 us
    all_to_all x1, starting transfers between devices, body(): lax.all_to_all(spectrum.reshape(256, 16, LANES), AXES, 0, 0, tiled=True)  13.3 us
    pallas_call x1, Pallas kernels, y_transform(): pl.pallas_call(y_kernel, out_shape=jax.ShapeDtypeStruct((2, 8, PLANES, LE...  5.09 us
    pallas_call x1, Pallas kernels, x_transform(): pl.pallas_call(x_kernel, out_shape=jax.ShapeDtypeStruct((LENGTH, LANES),...  3.48 us
    unnamed x20, local copies, waits for them, and re-layouts  2.95 us
  transfers between devices with their start and end apart: 1, of which 1 were waited for; matrix products, arithmetic and copies ran while one was open for 0% of the time, Pallas kernels for 0%

profile of v2, /device:TPU:1, one launch (start us, length us, event | category | flops | bytes accessed | tf_op | source)
XLA Modules:
  0.0 141.0 jit_solution(12147623858958871190)
XLA Ops:
  0.0 0.0 copy-start
  0.0 1.6 %copy-done = f32[64,8192]{1,0:T(8,128)S(1)} copy-done((f32[64,8192]{1,0:T(8,128)S(1)}, f32[64,8192]{1,0:T(8,128)}, u32[]{:S(2)}) %copy-start) | copy-done | bytes 2097176
  1.6 0.3 bitcast_bitcast_fusion
  1.9 0.0 copy-start.2
  1.9 0.0 copy-start.4
  1.9 62.1 %all_to_all.10 = f32[64,64,128]{2,1,0:T(8,128)S(1)} all-to-all(f32[64,64,128]{2,1,0:T(8,128)S(1)} %bitcast_bitcast_fusion), channel_id=1, replica_groups=mesh['zh'=4,'x'=4,'y'=4,'zl'=2,'core'=2] {'zh','x','y'}, dimensions={0} | all-to-all | bytes 4194304 | tf_op jit(solution)/shard_map/all_to_all | solution.py:216
  64.0 0.0 copy-done.2
  64.0 0.0 copy-done.4
  64.0 3.5 %x_transform.1 = f32[4096,128]{1,0:T(8,128)S(1)} custom-call(bf16[64,192]{1,0:T(8,128)(2,1)S(1)} %copy-done.4, bf16[33,128,192]{2,1,0:T(8,128)(2,1)S(1)} %copy-done.2, f32[4096,128]{1,0:T(8,128)S(1)} %bitcast.12), custom_call_target="tpu_custom_call" | custom-call | tf_op jit(solution)/shard_map/x_transform/pallas_call | solution.py:106
  67.5 0.0 copy-start.1
  67.5 1.3 copy-done.1
  68.8 0.0 copy-start.3
  68.8 0.0 copy-start.5
  68.8 0.0 copy-start.8
  68.8 0.0 copy-start.9
  68.8 13.3 %all-to-all-start.1 = ((f32[256,16,128]{2,1,0:T(8,128)}), f32[256,16,128]{2,1,0:T(8,128)}, u32[]{:S(2)}, u32[]{:S(2)}) async-start(f32[256,16,128]{2,1,0:T(8,128)} %bitcast.11), calls=%async_computation.1 | async-start | bytes 4194304 | tf_op jit(solution)/shard_map/all_to_all | solution.py:218
  82.1 53.8 %all-to-all-done.1 = f32[256,16,128]{2,1,0:T(8,128)} async-done(((f32[256,16,128]{2,1,0:T(8,128)}), f32[256,16,128]{2,1,0:T(8,128)}, u32[]{:S(2)}, u32[]{:S(2)}) %all-to-all-start.1) | async-done | bytes 2097184 | tf_op jit(solution)/shard_map/all_to_all | solution.py:218
  135.9 0.0 copy-done.3
  135.9 0.0 copy-done.5
  135.9 0.0 copy-done.6
  135.9 0.0 copy-done.7
  135.9 0.0 copy-done.8
  135.9 0.0 copy-done.9
  135.9 5.1 %y_transform.1 = f32[2,8,8,4096]{3,2,1,0:T(8,128)} custom-call(s32[1]{0:T(128)} %bitcast.place_ref, f32[2048]{0:T(1024)S(1)} %copy-done.8, f32[8]{0:T(128)S(1)} %copy-done.9, bf16[768,512]{1,0:T(8,128)(2,1)S(1)} %copy-done.3, f32[16,256]{1,0:T(8,128)S(1)} %copy-done.7, f32[16,256]{1,0:T(8,128)S(1)} %copy-done.6, f32[16,256]{1,0:T(8,128)S(1)} %copy-done.5, ...), custom_call_target="tpu_custom_call" | custom-call | tf_op jit(solution)/shard_map/y_transform/pallas_call | solution.py:190
  (2 shorter events, 0.0 us)
Async XLA Ops:
  0.0 1.6 %copy-start = (f32[64,8192]{1,0:T(8,128)S(1)}, f32[64,8192]{1,0:T(8,128)}, u32[]{:S(2)}) copy-start(f32[64,8192]{1,0:T(8,128)} %param.9) | copy-start | bytes 6291460
  1.9 62.1 %copy-start.2 = (bf16[33,128,192]{2,1,0:T(8,128)(2,1)S(1)}, bf16[33,128,192]{2,1,0:T(8,128)(2,1)}, u32[]{:S(2)}) copy-start(bf16[33,128,192]{2,1,0:T(8,128)(2,1)} %constant.42.clone.section_ref) | copy-start | bytes 4866052
  1.9 62.1 %copy-start.4 = (bf16[64,192]{1,0:T(8,128)(2,1)S(1)}, bf16[64,192]{1,0:T(8,128)(2,1)}, u32[]{:S(2)}) copy-start(bf16[64,192]{1,0:T(8,128)(2,1)} %constant.41.clone.outer_ref) | copy-start | bytes 73732
  67.5 1.3 copy-start.1
  68.8 67.1 %copy-start.3 = (bf16[768,512]{1,0:T(8,128)(2,1)S(1)}, bf16[768,512]{1,0:T(8,128)(2,1)}, u32[]{:S(2)}) copy-start(bf16[768,512]{1,0:T(8,128)(2,1)} %constant.44.clone.table_ref) | copy-start | bytes 2359300
  68.8 67.1 %copy-start.5 = (f32[16,256]{1,0:T(8,128)S(1)}, f32[16,256]{1,0:T(8,128)}, u32[]{:S(2)}) copy-start(f32[16,256]{1,0:T(8,128)} %constant.47.clone.symbol_ref) | copy-start | bytes 49156
  68.8 67.1 %copy-start.6 = (f32[16,256]{1,0:T(8,128)S(1)}, f32[16,256]{1,0:T(8,128)}, u32[]{:S(2)}) copy-start(f32[16,256]{1,0:T(8,128)} %constant.46.clone.sine_ref) | copy-start | bytes 49156
  68.8 67.1 %copy-start.7 = (f32[16,256]{1,0:T(8,128)S(1)}, f32[16,256]{1,0:T(8,128)}, u32[]{:S(2)}) copy-start(f32[16,256]{1,0:T(8,128)} %constant.45.clone.cosine_ref) | copy-start | bytes 49156
  68.8 67.1 %copy-start.8 = (f32[2048]{0:T(1024)S(1)}, f32[2048]{0:T(1024)}, u32[]{:S(2)}) copy-start(f32[2048]{0:T(1024)} %constant.43.clone.symbol_x_ref) | copy-start | bytes 24580
  68.8 67.1 %copy-start.9 = (f32[8]{0:T(128)S(1)}, f32[8]{0:T(128)}, u32[]{:S(2)}) copy-start(f32[8]{0:T(128)} %kz_ref.1) | copy-start | bytes 100
  68.8 67.1 %all-to-all-start.1 = ((f32[256,16,128]{2,1,0:T(8,128)}), f32[256,16,128]{2,1,0:T(8,128)}, u32[]{:S(2)}, u32[]{:S(2)}) async-start(f32[256,16,128]{2,1,0:T(8,128)} %bitcast.11), calls=%async_computation.1 | async-start | bytes 4194304 | tf_op jit(solution)/shard_map/all_to_all | solution.py:218

commit v3 on v2

--- a/solution.py
+++ b/solution.py
@@ -67,11 +67,13 @@
     )
 
 
-def x_kernel(outer_ref, section_ref, lines_ref, out_ref, mixed_ref):
+def x_kernel(place_ref, outer_ref, section_ref, lines_ref, out_ref, mixed_ref, staged_ref):
     outer = outer_ref[...]
+    for a in range(ROOT):
+        staged_ref[a * PITCH : a * PITCH + ROOT, :] = lines_ref[a * ROOT : (a + 1) * ROOT, :]
     for b in range(0, ROOT, 2):
         pair = jnp.concatenate(
-            [lines_ref[pl.ds(b + i, ROOT, stride=ROOT), :] for i in range(2)], axis=1
+            [staged_ref[pl.ds(b + i, ROOT, stride=PITCH), :] for i in range(2)], axis=1
         )
         mixed = jnp.dot(outer, split_data(pair, 0, "hlh"), preferred_element_type=jnp.float32)
         for i in range(2):
@@ -79,8 +81,7 @@
     count = KEPT // ROOT
 
     def store(k1, part, values):
-        start = (k1 // 8) * 16 + part * 8 + k1 % 8
-        out_ref[pl.ds(start, count, stride=LANES), :] = values
+        staged_ref[(k1 * 2 + part) * 36 : (k1 * 2 + part) * 36 + count, :] = values
 
     for k1 in range(ROOT // 2 + 1):
         real = mixed_ref[k1 * PITCH : k1 * PITCH + ROOT, :]
@@ -99,17 +100,23 @@
             result = jnp.dot(section, split_data(real, 0, "hlh"), preferred_element_type=jnp.float32)
             store(k1, 0, result[:count])
             store(k1, 1, -result[count:])
-
-
-def x_transform(lines):
+    for k2 in range(count):
+        for high in range(8):
+            for part in range(2):
+                at = (k2 * 8 + high) * 16 + part * 8
+                out_ref[at : at + 8, :] = staged_ref[pl.ds((high * 16 + part) * 36 + k2, 8, stride=72), :]
+
+
+def x_transform(lines, place):
     outer, sections = x_tables()
     return pl.pallas_call(
         x_kernel,
         out_shape=jax.ShapeDtypeStruct((LENGTH, LANES), jnp.float32),
-        scratch_shapes=[pltpu.VMEM((ROOT * PITCH, LANES), jnp.float32)],
+        in_specs=[pl.BlockSpec(memory_space=pltpu.SMEM)] + [pl.BlockSpec(memory_space=pltpu.VMEM)] * 3,
+        scratch_shapes=[pltpu.VMEM((ROOT * PITCH, LANES), jnp.float32)] * 2,
         compiler_params=pltpu.CompilerParams(vmem_limit_bytes=40 << 20),
         name="x_transform",
-    )(jnp.asarray(outer), jnp.asarray(sections), lines)
+    )(place, jnp.asarray(outer), jnp.asarray(sections), lines)
 
 
 def add(p, q):
@@ -147,18 +154,20 @@
     return out
 
 
-def y_kernel(place_ref, symbol_x_ref, kz_ref, table_ref, cosine_ref, sine_ref, symbol_ref, lines_ref, out_ref, done_ref, sent):
+def y_kernel(place_ref, symbol_x_ref, kz_ref, table_ref, cosine_ref, sine_ref, symbol_ref, lines_ref, out_ref, done_ref, staged_ref, sent):
     table = table_ref[...]
     scale = -1.0 / math.sqrt(LENGTH * LENGTH)
     row = lax.broadcasted_iota(jnp.int32, (PLANES, 256), 0)
     kz = jnp.zeros((PLANES, 256), jnp.float32)
     for p in range(PLANES):
         kz = jnp.where(row == p, kz_ref[p], kz)
+    for source in range(256):
+        staged_ref[source * 24 : source * 24 + 16, :] = lines_ref[source * 16 : source * 16 + 16, :]
     copies = []
     for j in range(8):
         rows = []
         for part in range(2):
-            values = lines_ref[pl.ds(part * 8 + j, 256, stride=16), :]
+            values = staged_ref[pl.ds(part * 8 + j, 256, stride=24), :]
             rows.append(split_data(values.T, 1, "hlh"))
         product = jnp.dot(jnp.concatenate(rows, axis=0), table, preferred_element_type=jnp.float32)
         values = []
@@ -194,6 +203,7 @@
         out_specs=pl.BlockSpec(memory_space=pl.ANY),
         scratch_shapes=[
             pltpu.VMEM((8, 2, PLANES, LENGTH), jnp.float32),
+            pltpu.VMEM((256 * 24, LANES), jnp.float32),
             pltpu.SemaphoreType.DMA((8,)),
         ],
         compiler_params=pltpu.CompilerParams(vmem_limit_bytes=40 << 20),
@@ -214,7 +224,7 @@
     place = jnp.stack([lax.axis_index(AXES)]).astype(jnp.int32)
     blocks = jnp.transpose(density.reshape(ROOT, ROOT, LANES), (1, 0, 2))
     lines = lax.all_to_all(blocks, AXES[:3], 0, 0, tiled=True)
-    spectrum = x_transform(lines.reshape(LENGTH, LANES))
+    spectrum = x_transform(lines.reshape(LENGTH, LANES), place)
     lines = lax.all_to_all(spectrum.reshape(256, 16, LANES), AXES, 0, 0, tiled=True)
     return y_transform(lines.reshape(LENGTH, LANES), place, kz_square)
 

time: 141 us -> 142 us (level)
  waiting for transfers between devices: 53.8 us -> 46.9 us
  blocking collectives: 62.1 us -> 66.7 us
  starting transfers between devices: 13.3 us -> 15.5 us
  local copies, waits for them, and re-layouts: 3.21 us -> 4.84 us
    all_to_all x1, waiting for transfers between devices: 53.8 us -> 46.9 us  [body(): lines = lax.all_to_all(blocks, AXES[:3], 0, 0, tiled=True)]
    all_to_all x1, blocking collectives: 62.1 us -> 66.7 us  [body(): lax.all_to_all(spectrum.reshape(256, 16, LANES), AXES, 0, 0, tiled=True)]
    all_to_all x1, starting transfers between devices: 13.3 us -> 15.5 us  [body(): lines = lax.all_to_all(blocks, AXES[:3], 0, 0, tiled=True)]
    unnamed x20 -> x18, local copies, waits for them, and re-layouts: 2.95 us -> 3.25 us
where the time goes in v3:
time: 142 us; the launch traced here: 141 us
  blocking collectives  66.7 us (47%)
  waiting for transfers between devices  46.9 us (33%)
  starting transfers between devices  15.5 us (11%)
  Pallas kernels  7.4 us (5%)
  local copies, waits for them, and re-layouts  4.84 us (3%)
    all_to_all x1, blocking collectives, body(): lax.all_to_all(spectrum.reshape(256, 16, LANES), AXES, 0, 0, tiled=True)  66.7 us
    all_to_all x1, waiting for transfers between devices, body(): lines = lax.all_to_all(blocks, AXES[:3], 0, 0, tiled=True)  46.9 us
    all_to_all x1, starting transfers between devices, body(): lines = lax.all_to_all(blocks, AXES[:3], 0, 0, tiled=True)  15.5 us
    pallas_call x1, Pallas kernels, y_transform(): pl.pallas_call(y_kernel, out_shape=jax.ShapeDtypeStruct((2, 8, PLANES, LE...  3.87 us
    pallas_call x1, Pallas kernels, x_transform(): pl.pallas_call(x_kernel, out_shape=jax.ShapeDtypeStruct((LENGTH, LANES),...  3.53 us
    unnamed x18, local copies, waits for them, and re-layouts  3.25 us
  transfers between devices with their start and end apart: 1, of which 1 were waited for; matrix products, arithmetic and copies ran while one was open for 0% of the time, Pallas kernels for 0%

profile of v3, /device:TPU:1, one launch (start us, length us, event | category | flops | bytes accessed | tf_op | source)
XLA Modules:
  0.0 141.5 jit_solution(2246960618846167732)
XLA Ops:
  0.0 0.0 copy-start
  0.0 1.6 %copy-done = f32[64,8192]{1,0:T(8,128)S(1)} copy-done((f32[64,8192]{1,0:T(8,128)S(1)}, f32[64,8192]{1,0:T(8,128)}, u32[]{:S(2)}) %copy-start) | copy-done | bytes 2097176
  1.6 1.6 %bitcast_bitcast_fusion = f32[64,64,128]{2,1,0:T(8,128)} fusion(f32[64,8192]{1,0:T(8,128)S(1)} %copy-done), kind=kLoop, calls=%fused_computation | loop fusion | bytes 4194304 | tf_op jit(solution)/shard_map/transpose | solution.py:225
  3.2 0.0 copy-start.3
  3.2 15.5 %all-to-all-start = ((f32[64,64,128]{2,1,0:T(8,128)}), f32[64,64,128]{2,1,0:T(8,128)}, u32[]{:S(2)}, u32[]{:S(2)}) async-start(f32[64,64,128]{2,1,0:T(8,128)} %bitcast_bitcast_fusion), calls=%async_computation | async-start | bytes 4194304 | tf_op jit(solution)/shard_map/all_to_all | solution.py:226
  18.7 46.9 %all-to-all-done = f32[64,64,128]{2,1,0:T(8,128)} async-done(((f32[64,64,128]{2,1,0:T(8,128)}), f32[64,64,128]{2,1,0:T(8,128)}, u32[]{:S(2)}, u32[]{:S(2)}) %all-to-all-start) | async-done | bytes 2097184 | tf_op jit(solution)/shard_map/all_to_all | solution.py:226
  65.6 0.0 copy-done.3
  65.6 0.0 copy-start.1
  65.6 1.6 %copy-done.1 = bf16[33,128,192]{2,1,0:T(8,128)(2,1)S(1)} copy-done((bf16[33,128,192]{2,1,0:T(8,128)(2,1)S(1)}, bf16[33,128,192]{2,1,0:T(8,128)(2,1)}, u32[]{:S(2)}) %copy-start.1) | copy-done | bytes 1622040
  67.2 3.5 %x_transform.1 = f32[4096,128]{1,0:T(8,128)S(1)} custom-call(s32[1]{0:T(128)} %bitcast.place_ref, bf16[64,192]{1,0:T(8,128)(2,1)S(1)} %copy-done.3, bf16[33,128,192]{2,1,0:T(8,128)(2,1)S(1)} %copy-done.1, f32[4096,128]{1,0:T(8,128)} %bitcast.2.lines_ref), custom_call_target="tpu_custom_call" | custom-call | tf_op jit(solution)/shard_map/x_transform/pallas_call | solution.py:112
  70.7 0.0 copy-start.2
  70.7 0.0 copy-start.4
  70.8 0.0 copy-start.5
  70.8 0.0 copy-start.6
  70.8 0.0 copy-start.7
  70.8 0.0 copy-start.8
  70.8 66.7 %all_to_all.10 = f32[256,16,128]{2,1,0:T(8,128)S(1)} all-to-all(f32[256,16,128]{2,1,0:T(8,128)S(1)} %bitcast.11), channel_id=1, replica_groups=mesh['zh'=4,'x'=4,'y'=4,'zl'=2,'core'=2] {'zh','x','y','zl','core'}, dimensions={0} | all-to-all | bytes 4194304 | tf_op jit(solution)/shard_map/all_to_all | solution.py:228
  137.5 0.0 copy-done.2
  137.5 0.0 copy-done.4
  137.6 0.0 copy-done.5
  137.6 0.0 copy-done.6
  137.6 0.0 copy-done.7
  137.6 0.0 copy-done.8
  137.6 3.9 %y_transform.1 = f32[2,8,8,4096]{3,2,1,0:T(8,128)} custom-call(s32[1]{0:T(128)} %bitcast.place_ref, f32[2048]{0:T(1024)S(1)} %copy-done.7, f32[8]{0:T(128)S(1)} %copy-done.8, bf16[768,512]{1,0:T(8,128)(2,1)S(1)} %copy-done.2, f32[16,256]{1,0:T(8,128)S(1)} %copy-done.6, f32[16,256]{1,0:T(8,128)S(1)} %copy-done.5, f32[16,256]{1,0:T(8,128)S(1)} %copy-done.4, ...), custom_call_target="tpu_custom_call" | custom-call | tf_op jit(solution)/shard_map/y_transform/pallas_call | solution.py:199
Async XLA Ops:
  0.0 1.6 %copy-start = (f32[64,8192]{1,0:T(8,128)S(1)}, f32[64,8192]{1,0:T(8,128)}, u32[]{:S(2)}) copy-start(f32[64,8192]{1,0:T(8,128)} %param.9) | copy-start | bytes 6291460
  3.2 62.4 %copy-start.3 = (bf16[64,192]{1,0:T(8,128)(2,1)S(1)}, bf16[64,192]{1,0:T(8,128)(2,1)}, u32[]{:S(2)}) copy-start(bf16[64,192]{1,0:T(8,128)(2,1)} %constant.41.clone.outer_ref) | copy-start | bytes 73732
  3.2 62.4 %all-to-all-start = ((f32[64,64,128]{2,1,0:T(8,128)}), f32[64,64,128]{2,1,0:T(8,128)}, u32[]{:S(2)}, u32[]{:S(2)}) async-start(f32[64,64,128]{2,1,0:T(8,128)} %bitcast_bitcast_fusion), calls=%async_computation | async-start | bytes 4194304 | tf_op jit(solution)/shard_map/all_to_all | solution.py:226
  65.6 1.6 %copy-start.1 = (bf16[33,128,192]{2,1,0:T(8,128)(2,1)S(1)}, bf16[33,128,192]{2,1,0:T(8,128)(2,1)}, u32[]{:S(2)}) copy-start(bf16[33,128,192]{2,1,0:T(8,128)(2,1)} %constant.42.clone.section_ref) | copy-start | bytes 4866052
  70.7 66.8 %copy-start.2 = (bf16[768,512]{1,0:T(8,128)(2,1)S(1)}, bf16[768,512]{1,0:T(8,128)(2,1)}, u32[]{:S(2)}) copy-start(bf16[768,512]{1,0:T(8,128)(2,1)} %constant.44.clone.table_ref) | copy-start | bytes 2359300
  70.7 66.8 %copy-start.4 = (f32[16,256]{1,0:T(8,128)S(1)}, f32[16,256]{1,0:T(8,128)}, u32[]{:S(2)}) copy-start(f32[16,256]{1,0:T(8,128)} %constant.47.clone.symbol_ref) | copy-start | bytes 49156
  70.8 66.8 %copy-start.5 = (f32[16,256]{1,0:T(8,128)S(1)}, f32[16,256]{1,0:T(8,128)}, u32[]{:S(2)}) copy-start(f32[16,256]{1,0:T(8,128)} %constant.46.clone.sine_ref) | copy-start | bytes 49156
  70.8 66.8 %copy-start.6 = (f32[16,256]{1,0:T(8,128)S(1)}, f32[16,256]{1,0:T(8,128)}, u32[]{:S(2)}) copy-start(f32[16,256]{1,0:T(8,128)} %constant.45.clone.cosine_ref) | copy-start | bytes 49156
  70.8 66.8 %copy-start.7 = (f32[2048]{0:T(1024)S(1)}, f32[2048]{0:T(1024)}, u32[]{:S(2)}) copy-start(f32[2048]{0:T(1024)} %constant.43.clone.symbol_x_ref) | copy-start | bytes 24580
  70.8 66.8 %copy-start.8 = (f32[8]{0:T(128)S(1)}, f32[8]{0:T(128)}, u32[]{:S(2)}) copy-start(f32[8]{0:T(128)} %kz_ref.1) | copy-start | bytes 100

commit v4 on v3

--- a/solution.py
+++ b/solution.py
@@ -18,6 +18,7 @@
 PITCH = 72
 PLANES = 8
 AXES = ("zh", "x", "y", "zl", "core")
+SIZES = (4, 4, 4, 2, 2)
 
 
 def split_table(table, axis, order):
@@ -67,7 +68,7 @@
     )
 
 
-def x_kernel(place_ref, outer_ref, section_ref, lines_ref, out_ref, mixed_ref, staged_ref):
+def x_kernel(outer_ref, section_ref, lines_ref, out_ref, mixed_ref, staged_ref):
     outer = outer_ref[...]
     for a in range(ROOT):
         staged_ref[a * PITCH : a * PITCH + ROOT, :] = lines_ref[a * ROOT : (a + 1) * ROOT, :]
@@ -107,16 +108,15 @@
                 out_ref[at : at + 8, :] = staged_ref[pl.ds((high * 16 + part) * 36 + k2, 8, stride=72), :]
 
 
-def x_transform(lines, place):
+def x_transform(lines):
     outer, sections = x_tables()
     return pl.pallas_call(
         x_kernel,
         out_shape=jax.ShapeDtypeStruct((LENGTH, LANES), jnp.float32),
-        in_specs=[pl.BlockSpec(memory_space=pltpu.SMEM)] + [pl.BlockSpec(memory_space=pltpu.VMEM)] * 3,
         scratch_shapes=[pltpu.VMEM((ROOT * PITCH, LANES), jnp.float32)] * 2,
         compiler_params=pltpu.CompilerParams(vmem_limit_bytes=40 << 20),
         name="x_transform",
-    )(place, jnp.asarray(outer), jnp.asarray(sections), lines)
+    )(jnp.asarray(outer), jnp.asarray(sections), lines)
 
 
 def add(p, q):
@@ -154,7 +154,7 @@
     return out
 
 
-def y_kernel(place_ref, symbol_x_ref, kz_ref, table_ref, cosine_ref, sine_ref, symbol_ref, lines_ref, out_ref, done_ref, staged_ref, sent):
+def y_kernel(symbol_x_ref, kz_ref, table_ref, cosine_ref, sine_ref, symbol_ref, lines_ref, out_ref, done_ref, staged_ref, sent):
     table = table_ref[...]
     scale = -1.0 / math.sqrt(LENGTH * LENGTH)
     row = lax.broadcasted_iota(jnp.int32, (PLANES, 256), 0)
@@ -163,6 +163,9 @@
         kz = jnp.where(row == p, kz_ref[p], kz)
     for source in range(256):
         staged_ref[source * 24 : source * 24 + 16, :] = lines_ref[source * 16 : source * 16 + 16, :]
+    device = 0
+    for axis, size in zip(AXES, SIZES):
+        device = device * size + lax.axis_index(axis)
     copies = []
     for j in range(8):
         rows = []
@@ -180,7 +183,7 @@
                 cosine, sine_part = cosine_ref[n : n + 1, :], sine_ref[n : n + 1, :]
                 real, imag = real * cosine - imag * sine_part, imag * cosine + real * sine_part
             values.append((real, imag))
-        shift = kz + symbol_x_ref[place_ref[0] * 8 + j]
+        shift = kz + symbol_x_ref[device * 8 + j]
         for k, (real, imag) in enumerate(sixteen(values)):
             factor = scale / (shift + symbol_ref[k : k + 1, :])
             done_ref[j, 0, :, k * 256 : (k + 1) * 256] = real * factor
@@ -191,7 +194,7 @@
         copy.wait()
 
 
-def y_transform(lines, place, kz_square):
+def y_transform(lines, kz_square):
     table, cosine, sine_part, symbol = y_tables()
     symbol_x = (4.0 * np.sin(np.pi * np.arange(KEPT) / LENGTH) ** 2).astype(np.float32)
     vmem = pl.BlockSpec(memory_space=pltpu.VMEM)
@@ -199,7 +202,7 @@
     return pl.pallas_call(
         y_kernel,
         out_shape=jax.ShapeDtypeStruct((2, 8, PLANES, LENGTH), jnp.float32),
-        in_specs=[smem] * 3 + [vmem] * 5,
+        in_specs=[smem] * 2 + [vmem] * 5,
         out_specs=pl.BlockSpec(memory_space=pl.ANY),
         scratch_shapes=[
             pltpu.VMEM((8, 2, PLANES, LENGTH), jnp.float32),
@@ -209,7 +212,6 @@
         compiler_params=pltpu.CompilerParams(vmem_limit_bytes=40 << 20),
         name="y_transform",
     )(
-        place,
         jnp.asarray(symbol_x),
         kz_square,
         jnp.asarray(table),
@@ -221,16 +223,15 @@
 
 
 def body(density, kz_square):
-    place = jnp.stack([lax.axis_index(AXES)]).astype(jnp.int32)
     blocks = jnp.transpose(density.reshape(ROOT, ROOT, LANES), (1, 0, 2))
     lines = lax.all_to_all(blocks, AXES[:3], 0, 0, tiled=True)
-    spectrum = x_transform(lines.reshape(LENGTH, LANES), place)
+    spectrum = x_transform(lines.reshape(LENGTH, LANES))
     lines = lax.all_to_all(spectrum.reshape(256, 16, LANES), AXES, 0, 0, tiled=True)
-    return y_transform(lines.reshape(LENGTH, LANES), place, kz_square)
+    return y_transform(lines.reshape(LENGTH, LANES), kz_square)
 
 
 def solution(mesh):
-    fine = Mesh(mesh.devices.reshape(4, 4, 4, 2, 2), AXES)
+    fine = Mesh(mesh.devices.reshape(SIZES), AXES)
     in_specs = (P(AXES[:3], AXES[3:]), P())
     out_specs = P(None, AXES, None, None)
     return jax.shard_map(body, mesh=fine, in_specs=in_specs, out_specs=out_specs, check_vma=False)

time: 142 us -> 137 us (0.965)
  blocking collectives: 66.7 us -> 129 us
  waiting for transfers between devices: 46.9 us -> 0 us
  starting transfers between devices: 15.5 us -> 0 us
  local copies, waits for them, and re-layouts: 4.84 us -> 1.91 us
  Pallas kernels: 7.4 us -> 5.98 us
    all_to_all x0 -> x1, blocking collectives: none -> 62.1 us  [body(): lines = lax.all_to_all(blocks, AXES[:3], 0, 0, tiled=True)]
    all_to_all x1 -> x0, waiting for transfers between devices: 46.9 us -> none  [body(): lines = lax.all_to_all(blocks, AXES[:3], 0, 0, tiled=True)]
    all_to_all x1 -> x0, starting transfers between devices: 15.5 us -> none  [body(): lines = lax.all_to_all(blocks, AXES[:3], 0, 0, tiled=True)]
    unnamed x18, local copies, waits for them, and re-layouts: 3.25 us -> 1.65 us
    pallas_call x1, Pallas kernels: 3.53 us -> 1.95 us  [x_transform(): pl.pallas_call(x_kernel, out_shape=jax.ShapeDtypeStruct((LENGTH, LANES),...]
  transfers between devices with their start and end apart: 1 -> 0, of which waited for: 1 -> 0; matrix products, arithmetic and copies ran while one was open for 0% -> 0% of each run, Pallas kernels for 0% -> 0%
where the time goes in v4:
time: 137 us
  blocking collectives  129 us (94%)
  Pallas kernels  5.98 us (4%)
  local copies, waits for them, and re-layouts  1.91 us (1%)
    all_to_all x1, blocking collectives, body(): lax.all_to_all(spectrum.reshape(256, 16, LANES), AXES, 0, 0, tiled=True)  66.7 us
    all_to_all x1, blocking collectives, body(): lines = lax.all_to_all(blocks, AXES[:3], 0, 0, tiled=True)  62.1 us
    pallas_call x1, Pallas kernels, y_transform(): pl.pallas_call(y_kernel, out_shape=jax.ShapeDtypeStruct((2, 8, PLANES, LE...  4.03 us

profile of v4, /device:TPU:1, one launch (start us, length us, event | category | flops | bytes accessed | tf_op | source)
XLA Modules:
  0.0 136.8 jit_solution(14095629748652383408)
XLA Ops:
  0.0 0.0 copy-start
  0.0 1.6 %copy-done = f32[64,8192]{1,0:T(8,128)S(1)} copy-done((f32[64,8192]{1,0:T(8,128)S(1)}, f32[64,8192]{1,0:T(8,128)}, u32[]{:S(2)}) %copy-start) | copy-done | bytes 2097176
  1.6 0.3 bitcast_bitcast_fusion
  1.9 0.0 copy-start.1
  1.9 0.0 copy-start.3
  1.9 62.1 %all_to_all.10 = f32[64,64,128]{2,1,0:T(8,128)S(1)} all-to-all(f32[64,64,128]{2,1,0:T(8,128)S(1)} %bitcast_bitcast_fusion), channel_id=1, replica_groups=mesh['zh'=4,'x'=4,'y'=4,'zl'=2,'core'=2] {'zh','x','y'}, dimensions={0} | all-to-all | bytes 4194304 | tf_op jit(solution)/shard_map/all_to_all | solution.py:227
  64.0 0.0 copy-done.1
  64.0 0.0 copy-done.3
  64.0 2.0 %x_transform.1 = f32[4096,128]{1,0:T(8,128)S(1)} custom-call(bf16[64,192]{1,0:T(8,128)(2,1)S(1)} %copy-done.3, bf16[33,128,192]{2,1,0:T(8,128)(2,1)S(1)} %copy-done.1, f32[4096,128]{1,0:T(8,128)S(1)} %bitcast.10), custom_call_target="tpu_custom_call" | custom-call | tf_op jit(solution)/shard_map/x_transform/pallas_call | solution.py:113
  65.9 0.0 copy-start.2
  65.9 0.0 copy-start.4
  66.0 0.0 copy-start.5
  66.0 0.0 copy-start.6
  66.0 0.0 copy-start.7
  66.0 0.0 copy-start.8
  66.0 66.7 %all_to_all.11 = f32[256,16,128]{2,1,0:T(8,128)S(1)} all-to-all(f32[256,16,128]{2,1,0:T(8,128)S(1)} %bitcast.11), channel_id=1, replica_groups=mesh['zh'=4,'x'=4,'y'=4,'zl'=2,'core'=2] {'zh','x','y','zl','core'}, dimensions={0} | all-to-all | bytes 4194304 | tf_op jit(solution)/shard_map/all_to_all | solution.py:229
  132.7 0.0 copy-done.2
  132.8 0.0 copy-done.4
  132.8 0.0 copy-done.5
  132.8 0.0 copy-done.6
  132.8 0.0 copy-done.7
  132.8 0.0 copy-done.8
  132.8 4.0 %y_transform.1 = f32[2,8,8,4096]{3,2,1,0:T(8,128)} custom-call(f32[2048]{0:T(1024)S(1)} %copy-done.7, f32[8]{0:T(128)S(1)} %copy-done.8, bf16[768,512]{1,0:T(8,128)(2,1)S(1)} %copy-done.2, f32[16,256]{1,0:T(8,128)S(1)} %copy-done.6, f32[16,256]{1,0:T(8,128)S(1)} %copy-done.5, f32[16,256]{1,0:T(8,128)S(1)} %copy-done.4, f32[4096,128]{1,0:T(8,128)S(1)} %bitcast.12), custom_call_target="tpu_custom_call" | custom-call | tf_op jit(solution)/shard_map/y_transform/pallas_call | solution.py:202
Async XLA Ops:
  0.0 1.6 %copy-start = (f32[64,8192]{1,0:T(8,128)S(1)}, f32[64,8192]{1,0:T(8,128)}, u32[]{:S(2)}) copy-start(f32[64,8192]{1,0:T(8,128)} %param.9) | copy-start | bytes 6291460
  1.9 62.1 %copy-start.1 = (bf16[33,128,192]{2,1,0:T(8,128)(2,1)S(1)}, bf16[33,128,192]{2,1,0:T(8,128)(2,1)}, u32[]{:S(2)}) copy-start(bf16[33,128,192]{2,1,0:T(8,128)(2,1)} %constant.15.clone.section_ref) | copy-start | bytes 4866052
  1.9 62.1 %copy-start.3 = (bf16[64,192]{1,0:T(8,128)(2,1)S(1)}, bf16[64,192]{1,0:T(8,128)(2,1)}, u32[]{:S(2)}) copy-start(bf16[64,192]{1,0:T(8,128)(2,1)} %constant.14.clone.outer_ref) | copy-start | bytes 73732
  65.9 66.8 %copy-start.2 = (bf16[768,512]{1,0:T(8,128)(2,1)S(1)}, bf16[768,512]{1,0:T(8,128)(2,1)}, u32[]{:S(2)}) copy-start(bf16[768,512]{1,0:T(8,128)(2,1)} %constant.17.clone.table_ref) | copy-start | bytes 2359300
  65.9 66.8 %copy-start.4 = (f32[16,256]{1,0:T(8,128)S(1)}, f32[16,256]{1,0:T(8,128)}, u32[]{:S(2)}) copy-start(f32[16,256]{1,0:T(8,128)} %constant.20.clone.symbol_ref) | copy-start | bytes 49156
  66.0 66.8 %copy-start.5 = (f32[16,256]{1,0:T(8,128)S(1)}, f32[16,256]{1,0:T(8,128)}, u32[]{:S(2)}) copy-start(f32[16,256]{1,0:T(8,128)} %constant.19.clone.sine_ref) | copy-start | bytes 49156
  66.0 66.8 %copy-start.6 = (f32[16,256]{1,0:T(8,128)S(1)}, f32[16,256]{1,0:T(8,128)}, u32[]{:S(2)}) copy-start(f32[16,256]{1,0:T(8,128)} %constant.18.clone.cosine_ref) | copy-start | bytes 49156
  66.0 66.8 %copy-start.7 = (f32[2048]{0:T(1024)S(1)}, f32[2048]{0:T(1024)}, u32[]{:S(2)}) copy-start(f32[2048]{0:T(1024)} %constant.16.clone.symbol_x_ref) | copy-start | bytes 24580
  66.0 66.8 %copy-start.8 = (f32[8]{0:T(128)S(1)}, f32[8]{0:T(128)}, u32[]{:S(2)}) copy-start(f32[8]{0:T(128)} %kz_ref.1) | copy-start | bytes 100

commit v5 on v4

--- a/solution.py
+++ b/solution.py
@@ -16,9 +16,11 @@
 ROOT = 64
 LANES = 128
 PITCH = 72
+ROWS = 32
 PLANES = 8
 AXES = ("zh", "x", "y", "zl", "core")
 SIZES = (4, 4, 4, 2, 2)
+LIMIT = pltpu.CompilerParams(vmem_limit_bytes=24 << 20)
 
 
 def split_table(table, axis, order):
@@ -68,10 +70,58 @@
     )
 
 
-def x_kernel(outer_ref, section_ref, lines_ref, out_ref, mixed_ref, staged_ref):
+def pack_kernel(density_ref, *out_refs):
+    zh = lax.axis_index("zh")
+    for dz in range(4):
+        base = ((zh + dz) & 3) * (16 * LANES)
+        for xy in range(16):
+            columns = pl.ds(pl.multiple_of(base + xy * LANES, LANES), LANES)
+            out_refs[dz][xy] = density_ref[:ROWS, columns]
+            out_refs[4][xy, dz] = density_ref[ROWS:, columns]
+
+
+def join_kernel(earlier_ref, *refs):
+    for slot, ref in enumerate(refs[:-1]):
+        refs[-1][:, slot] = ref[...]
+
+
+def split_kernel(in_ref, *out_refs):
+    for slot, ref in enumerate(out_refs):
+        ref[...] = in_ref[:, slot]
+
+
+def floats(*shape):
+    return pltpu.VMEM(shape, jnp.float32)
+
+
+def pack(density):
+    out_shape = [floats(16, ROWS, LANES)] * 4 + [floats(16, 4, ROWS, LANES)]
+    return pl.pallas_call(pack_kernel, out_shape=out_shape, name="pack", compiler_params=LIMIT)(density)
+
+
+def join(parts, earlier):
+    in_specs = [pl.BlockSpec(memory_space=pl.ANY)] + [pl.BlockSpec(memory_space=pltpu.VMEM)] * 4
+    return pl.pallas_call(
+        join_kernel, out_shape=floats(16, 4, ROWS, LANES), in_specs=in_specs, name="join", compiler_params=LIMIT
+    )(earlier, *parts)
+
+
+def split(whole):
+    return pl.pallas_call(
+        split_kernel, out_shape=[floats(16, ROWS, LANES)] * 4, name="split", compiler_params=LIMIT
+    )(whole)
+
+
+def x_kernel(outer_ref, section_ref, first_ref, *refs):
+    second_refs, (out_ref, mixed_ref, staged_ref) = refs[:4], refs[4:]
     outer = outer_ref[...]
-    for a in range(ROOT):
-        staged_ref[a * PITCH : a * PITCH + ROOT, :] = lines_ref[a * ROOT : (a + 1) * ROOT, :]
+    zh = lax.axis_index("zh")
+    for dz in range(4):
+        base = ((zh - dz) & 3) * (16 * PITCH)
+        for xy in range(16):
+            start = pl.multiple_of(base + xy * PITCH, 8)
+            staged_ref[pl.ds(start, ROWS), :] = first_ref[xy, dz]
+            staged_ref[pl.ds(start + ROWS, ROWS), :] = second_refs[dz][xy]
     for b in range(0, ROOT, 2):
         pair = jnp.concatenate(
             [staged_ref[pl.ds(b + i, ROOT, stride=PITCH), :] for i in range(2)], axis=1
@@ -108,15 +158,15 @@
                 out_ref[at : at + 8, :] = staged_ref[pl.ds((high * 16 + part) * 36 + k2, 8, stride=72), :]
 
 
-def x_transform(lines):
+def x_transform(first, second):
     outer, sections = x_tables()
     return pl.pallas_call(
         x_kernel,
         out_shape=jax.ShapeDtypeStruct((LENGTH, LANES), jnp.float32),
         scratch_shapes=[pltpu.VMEM((ROOT * PITCH, LANES), jnp.float32)] * 2,
-        compiler_params=pltpu.CompilerParams(vmem_limit_bytes=40 << 20),
+        compiler_params=LIMIT,
         name="x_transform",
-    )(jnp.asarray(outer), jnp.asarray(sections), lines)
+    )(jnp.asarray(outer), jnp.asarray(sections), first, *second)
 
 
 def add(p, q):
@@ -209,7 +259,7 @@
             pltpu.VMEM((256 * 24, LANES), jnp.float32),
             pltpu.SemaphoreType.DMA((8,)),
         ],
-        compiler_params=pltpu.CompilerParams(vmem_limit_bytes=40 << 20),
+        compiler_params=LIMIT,
         name="y_transform",
     )(
         jnp.asarray(symbol_x),
@@ -222,10 +272,25 @@
     )
 
 
+def around(parts):
+    arrived = list(parts)
+    for dz in (2, 1, 3):
+        arrived[dz] = lax.ppermute(parts[dz], "zh", [(i, (i + dz) % 4) for i in range(4)])
+    return arrived
+
+
+def across(whole):
+    inside = lax.axis_index("core") < SIZES[4]
+    return lax.cond(inside, lambda v: lax.all_to_all(v, ("x", "y"), 0, 0, tiled=True), lambda v: v, whole)
+
+
 def body(density, kz_square):
-    blocks = jnp.transpose(density.reshape(ROOT, ROOT, LANES), (1, 0, 2))
-    lines = lax.all_to_all(blocks, AXES[:3], 0, 0, tiled=True)
-    spectrum = x_transform(lines.reshape(LENGTH, LANES))
+    *first, second = pack(density)
+    first = around(first)
+    second = split(across(second))
+    first = across(join(first, second[0]))
+    second = around(second)
+    spectrum = x_transform(first, second)
     lines = lax.all_to_all(spectrum.reshape(256, 16, LANES), AXES, 0, 0, tiled=True)
     return y_transform(lines.reshape(LENGTH, LANES), kz_square)
 

time: 137 us -> 134 us (0.978)
  blocking collectives: 129 us -> 99.9 us
  starting transfers between devices: 0 us -> 15.7 us
  waiting for transfers between devices: 0 us -> 7.49 us
  Pallas kernels: 5.98 us -> 8.44 us
    all_to_all x1 -> x2, blocking collectives: 62.1 us -> 38.8 us  [across(): lax.all_to_all(v, ('x', 'y'), 0, 0, tiled=True)]
    ppermute x0 -> x6, starting transfers between devices: none -> 15.7 us  [around(): lax.ppermute(parts[dz], 'zh', [(i, (i + dz) % 4) for i in range(4)])]
    ppermute x0 -> x6, waiting for transfers between devices: none -> 7.49 us  [around(): lax.ppermute(parts[dz], 'zh', [(i, (i + dz) % 4) for i in range(4)])]
    all_to_all x1, blocking collectives: 66.7 us -> 61.1 us  [body(): lax.all_to_all(spectrum.reshape(256, 16, LANES), AXES, 0, 0, tiled=True)]
  transfers between devices with their start and end apart: 0 -> 6, of which waited for: 0 -> 1; matrix products, arithmetic and copies ran while one was open for 0% -> 0% of each run, Pallas kernels for 0% -> 1%
where the time goes in v5:
time: 134 us; the launch traced here: 133 us
  blocking collectives  99.9 us (75%)
  starting transfers between devices  15.7 us (12%)
  Pallas kernels  8.44 us (6%)
  waiting for transfers between devices  7.49 us (6%)
  local copies, waits for them, and re-layouts  1.83 us (1%)
    all_to_all x1, blocking collectives, body(): lax.all_to_all(spectrum.reshape(256, 16, LANES), AXES, 0, 0, tiled=True)  61.1 us
    all_to_all x2, blocking collectives, across(): lax.all_to_all(v, ('x', 'y'), 0, 0, tiled=True)  38.8 us
    ppermute x6, starting transfers between devices, around(): lax.ppermute(parts[dz], 'zh', [(i, (i + dz) % 4) for i in range(4)])  15.7 us
    ppermute x6, waiting for transfers between devices, around(): lax.ppermute(parts[dz], 'zh', [(i, (i + dz) % 4) for i in range(4)])  7.49 us
    pallas_call x1, Pallas kernels, y_transform(): pl.pallas_call(y_kernel, out_shape=jax.ShapeDtypeStruct((2, 8, PLANES, LE...  4.03 us
    pallas_call x1, Pallas kernels, x_transform(): pl.pallas_call(x_kernel, out_shape=jax.ShapeDtypeStruct((LENGTH, LANES),...  3.15 us
  transfers between devices with their start and end apart: 6, of which 1 were waited for; matrix products, arithmetic and copies ran while one was open for 0% of the time, Pallas kernels for 1%

profile of v5, /device:TPU:1, one launch (start us, length us, event | category | flops | bytes accessed | tf_op | source)
XLA Modules:
  0.0 133.4 jit_solution(12345066211397102164)
XLA Ops:
  0.0 1.6 %copy-done.1 = f32[64,8192]{1,0:T(8,128)S(1)} copy-done((f32[64,8192]{1,0:T(8,128)S(1)}, f32[64,8192]{1,0:T(8,128)}, u32[]{:S(2)}) %copy-start.1) | copy-done | bytes 2097176
  1.6 0.3 pack.1
  1.9 3.9 %collective-permute-start = (f32[16,32,128]{2,1,0:T(8,128)S(1)}, f32[16,32,128]{2,1,0:T(8,128)S(1)}, u32[]{:S(2)}, u32[]{:S(2)}) collective-permute-start(f32[16,32,128]{2,1,0:T(8,128)S(1)} %get-tuple-element.27), channel_id=1, source_target_pairs={{0,64},{64,128},{128,192},{192,0},{1,65},{65,129},{129,193},{193,1... | collective-permute-start | bytes 786440 | tf_op jit(solution)/shard_map/ppermute | solution.py:278
  5.8 5.1 %collective-permute-start.1 = (f32[16,32,128]{2,1,0:T(8,128)S(1)}, f32[16,32,128]{2,1,0:T(8,128)S(1)}, u32[]{:S(2)}, u32[]{:S(2)}) collective-permute-start(f32[16,32,128]{2,1,0:T(8,128)S(1)} %get-tuple-element.28), channel_id=1, source_target_pairs={{0,128},{64,192},{128,0},{192,64},{1,129},{65,193},{129,1},{193,65... | collective-permute-start | bytes 786440 | tf_op jit(solution)/shard_map/ppermute | solution.py:278
  10.9 2.4 %collective-permute-start.2 = (f32[16,32,128]{2,1,0:T(8,128)S(1)}, f32[16,32,128]{2,1,0:T(8,128)S(1)}, u32[]{:S(2)}, u32[]{:S(2)}) collective-permute-start(f32[16,32,128]{2,1,0:T(8,128)S(1)} %get-tuple-element.29), channel_id=1, source_target_pairs={{0,192},{64,0},{128,64},{192,128},{1,193},{65,1},{129,65},{193,129... | collective-permute-start | bytes 786440 | tf_op jit(solution)/shard_map/ppermute | solution.py:278
  13.3 21.5 %conditional.2 = (f32[16,4,32,128]{3,2,1,0:T(8,128)S(1)}) conditional(s32[]{:T(128)} %convert_element_type.4, f32[16,4,32,128]{3,2,1,0:T(8,128)S(1)} %get-tuple-element.24, f32[16,4,32,128]{3,2,1,0:T(8,128)S(1)} %get-tuple-element.24), branch_computations={%region_0.0_spmd, %region_1.0_spmd} | conditional | bytes 4194312 | solution.py:284
  13.3 0.1 copy.14
  13.4 21.4 %all_to_all.13 = f32[16,4,32,128]{3,2,1,0:T(8,128)S(1)} all-to-all(f32[16,4,32,128]{3,2,1,0:T(8,128)S(1)} %copy.14), channel_id=1, replica_groups=mesh['zh'=4,'x'=4,'y'=4,'zl'=2,'core'=2] {'x','y'}, dimensions={0} | all-to-all | bytes 2097152 | tf_op jit(solution)/shard_map/cond/branch_1_fun/all_to_all | solution.py:284
  34.7 0.9 split.1
  35.6 1.8 %collective-permute-start.4 = (f32[16,32,128]{2,1,0:T(8,128)}, f32[16,32,128]{2,1,0:T(8,128)}, u32[]{:S(2)}, u32[]{:S(2)}) collective-permute-start(f32[16,32,128]{2,1,0:T(8,128)} %get-tuple-element.31), channel_id=1, source_target_pairs={{0,128},{64,192},{128,0},{192,64},{1,129},{65,193},{129,1},{193,65... | collective-permute-start | bytes 786440 | tf_op jit(solution)/shard_map/ppermute | solution.py:278
  37.4 2.5 %collective-permute-start.5 = (f32[16,32,128]{2,1,0:T(8,128)}, f32[16,32,128]{2,1,0:T(8,128)}, u32[]{:S(2)}, u32[]{:S(2)}) collective-permute-start(f32[16,32,128]{2,1,0:T(8,128)} %get-tuple-element.32), channel_id=1, source_target_pairs={{0,192},{64,0},{128,64},{192,128},{1,193},{65,1},{129,65},{193,129... | collective-permute-start | bytes 786440 | tf_op jit(solution)/shard_map/ppermute | solution.py:278
  40.0 0.1 join.1
  40.0 0.0 copy-start
  40.0 0.0 copy-start.3
  40.1 17.5 %conditional.3 = (f32[16,4,32,128]{3,2,1,0:T(8,128)S(1)}) conditional(s32[]{:T(128)} %convert_element_type.4, f32[16,4,32,128]{3,2,1,0:T(8,128)S(1)} %join.1, f32[16,4,32,128]{3,2,1,0:T(8,128)S(1)} %join.1), branch_computations={%region_2.0_spmd, %region_3.0_spmd} | conditional | bytes 4194312 | solution.py:284
  40.1 0.1 copy.15
  40.2 17.4 %all_to_all.14 = f32[16,4,32,128]{3,2,1,0:T(8,128)S(1)} all-to-all(f32[16,4,32,128]{3,2,1,0:T(8,128)S(1)} %copy.15), channel_id=1, replica_groups=mesh['zh'=4,'x'=4,'y'=4,'zl'=2,'core'=2] {'x','y'}, dimensions={0} | all-to-all | bytes 2097152 | tf_op jit(solution)/shard_map/cond/branch_1_fun/all_to_all | solution.py:284
  57.6 7.5 %collective-permute-done.5.refs_3_ = f32[16,32,128]{2,1,0:T(8,128)} collective-permute-done((f32[16,32,128]{2,1,0:T(8,128)}, f32[16,32,128]{2,1,0:T(8,128)}, u32[]{:S(2)}, u32[]{:S(2)}) %collective-permute-start.5) | collective-permute-done | bytes 262176 | tf_op jit(solution)/shard_map/ppermute | solution.py:278
  65.1 3.2 %x_transform.1 = f32[4096,128]{1,0:T(8,128)S(1)} custom-call(bf16[64,192]{1,0:T(8,128)(2,1)S(1)} %copy-done.3, bf16[33,128,192]{2,1,0:T(8,128)(2,1)S(1)} %copy-done, f32[16,4,32,128]{3,2,1,0:T(8,128)S(1)} %get-tuple-element.34.first_ref, f32[16,32,128]{2,1,0:T(8,128)S(1)} %get-tuple-element.25.earlier_ref.refs_0_, ...), custom_call_target="tpu_custom_call" | custom-call | tf_op jit(solution)/shard_map/x_transform/pallas_call | solution.py:163
  68.2 0.0 copy-start.2
  68.2 0.0 copy-start.4
  68.3 0.0 copy-start.5
  68.3 61.1 %all_to_all.15 = f32[256,16,128]{2,1,0:T(8,128)S(1)} all-to-all(f32[256,16,128]{2,1,0:T(8,128)S(1)} %bitcast.2), channel_id=1, replica_groups=mesh['zh'=4,'x'=4,'y'=4,'zl'=2,'core'=2] {'zh','x','y','zl','core'}, dimensions={0} | all-to-all | bytes 4194304 | tf_op jit(solution)/shard_map/all_to_all | solution.py:294
  129.4 4.0 %y_transform.1 = f32[2,8,8,4096]{3,2,1,0:T(8,128)} custom-call(f32[2048]{0:T(1024)S(1)} %copy-done.7, f32[8]{0:T(128)S(1)} %copy-done.8, bf16[768,512]{1,0:T(8,128)(2,1)S(1)} %copy-done.2, f32[16,256]{1,0:T(8,128)S(1)} %copy-done.6, f32[16,256]{1,0:T(8,128)S(1)} %copy-done.5, f32[16,256]{1,0:T(8,128)S(1)} %copy-done.4, f32[4096,128]{1,0:T(8,128)S(1)} %bitcast.3), custom_call_target="tpu_custom_call" | custom-call | tf_op jit(solution)/shard_map/y_transform/pallas_call | solution.py:252
  (18 shorter events, 0.0 us)
Async XLA Ops:
  0.0 1.6 %copy-start.1 = (f32[64,8192]{1,0:T(8,128)S(1)}, f32[64,8192]{1,0:T(8,128)}, u32[]{:S(2)}) copy-start(f32[64,8192]{1,0:T(8,128)} %density_ref.1) | copy-start | bytes 6291460
  1.9 35.6 %collective-permute-start = (f32[16,32,128]{2,1,0:T(8,128)S(1)}, f32[16,32,128]{2,1,0:T(8,128)S(1)}, u32[]{:S(2)}, u32[]{:S(2)}) collective-permute-start(f32[16,32,128]{2,1,0:T(8,128)S(1)} %get-tuple-element.27), channel_id=1, source_target_pairs={{0,64},{64,128},{128,192},{192,0},{1,65},{65,129},{129,193},{193,1... | collective-permute-start | bytes 786440 | tf_op jit(solution)/shard_map/ppermute | solution.py:278
  5.8 34.2 %collective-permute-start.1 = (f32[16,32,128]{2,1,0:T(8,128)S(1)}, f32[16,32,128]{2,1,0:T(8,128)S(1)}, u32[]{:S(2)}, u32[]{:S(2)}) collective-permute-start(f32[16,32,128]{2,1,0:T(8,128)S(1)} %get-tuple-element.28), channel_id=1, source_target_pairs={{0,128},{64,192},{128,0},{192,64},{1,129},{65,193},{129,1},{193,65... | collective-permute-start | bytes 786440 | tf_op jit(solution)/shard_map/ppermute | solution.py:278
  10.9 29.1 %collective-permute-start.2 = (f32[16,32,128]{2,1,0:T(8,128)S(1)}, f32[16,32,128]{2,1,0:T(8,128)S(1)}, u32[]{:S(2)}, u32[]{:S(2)}) collective-permute-start(f32[16,32,128]{2,1,0:T(8,128)S(1)} %get-tuple-element.29), channel_id=1, source_target_pairs={{0,192},{64,0},{128,64},{192,128},{1,193},{65,1},{129,65},{193,129... | collective-permute-start | bytes 786440 | tf_op jit(solution)/shard_map/ppermute | solution.py:278
  35.6 21.9 %collective-permute-start.3 = (f32[16,32,128]{2,1,0:T(8,128)}, f32[16,32,128]{2,1,0:T(8,128)}, u32[]{:S(2)}, u32[]{:S(2)}) collective-permute-start(f32[16,32,128]{2,1,0:T(8,128)} %get-tuple-element.30), channel_id=1, source_target_pairs={{0,64},{64,128},{128,192},{192,0},{1,65},{65,129},{129,193},{193,1... | collective-permute-start | bytes 786440 | tf_op jit(solution)/shard_map/ppermute | solution.py:278
  35.6 21.9 %collective-permute-start.4 = (f32[16,32,128]{2,1,0:T(8,128)}, f32[16,32,128]{2,1,0:T(8,128)}, u32[]{:S(2)}, u32[]{:S(2)}) collective-permute-start(f32[16,32,128]{2,1,0:T(8,128)} %get-tuple-element.31), channel_id=1, source_target_pairs={{0,128},{64,192},{128,0},{192,64},{1,129},{65,193},{129,1},{193,65... | collective-permute-start | bytes 786440 | tf_op jit(solution)/shard_map/ppermute | solution.py:278
  37.4 27.6 %collective-permute-start.5 = (f32[16,32,128]{2,1,0:T(8,128)}, f32[16,32,128]{2,1,0:T(8,128)}, u32[]{:S(2)}, u32[]{:S(2)}) collective-permute-start(f32[16,32,128]{2,1,0:T(8,128)} %get-tuple-element.32), channel_id=1, source_target_pairs={{0,192},{64,0},{128,64},{192,128},{1,193},{65,1},{129,65},{193,129... | collective-permute-start | bytes 786440 | tf_op jit(solution)/shard_map/ppermute | solution.py:278
  40.0 25.0 %copy-start = (bf16[33,128,192]{2,1,0:T(8,128)(2,1)S(1)}, bf16[33,128,192]{2,1,0:T(8,128)(2,1)}, u32[]{:S(2)}) copy-start(bf16[33,128,192]{2,1,0:T(8,128)(2,1)} %constant.21.clone.section_ref) | copy-start | bytes 4866052
  40.0 25.0 %copy-start.3 = (bf16[64,192]{1,0:T(8,128)(2,1)S(1)}, bf16[64,192]{1,0:T(8,128)(2,1)}, u32[]{:S(2)}) copy-start(bf16[64,192]{1,0:T(8,128)(2,1)} %constant.20.clone.outer_ref) | copy-start | bytes 73732
  68.2 61.2 %copy-start.2 = (bf16[768,512]{1,0:T(8,128)(2,1)S(1)}, bf16[768,512]{1,0:T(8,128)(2,1)}, u32[]{:S(2)}) copy-start(bf16[768,512]{1,0:T(8,128)(2,1)} %constant.23.clone.table_ref) | copy-start | bytes 2359300
  68.2 61.1 %copy-start.4 = (f32[16,256]{1,0:T(8,128)S(1)}, f32[16,256]{1,0:T(8,128)}, u32[]{:S(2)}) copy-start(f32[16,256]{1,0:T(8,128)} %constant.26.clone.symbol_ref) | copy-start | bytes 49156
  68.3 61.1 %copy-start.5 = (f32[16,256]{1,0:T(8,128)S(1)}, f32[16,256]{1,0:T(8,128)}, u32[]{:S(2)}) copy-start(f32[16,256]{1,0:T(8,128)} %constant.25.clone.sine_ref) | copy-start | bytes 49156
  68.3 61.1 %copy-start.6 = (f32[16,256]{1,0:T(8,128)S(1)}, f32[16,256]{1,0:T(8,128)}, u32[]{:S(2)}) copy-start(f32[16,256]{1,0:T(8,128)} %constant.24.clone.cosine_ref) | copy-start | bytes 49156
  68.3 61.1 %copy-start.7 = (f32[2048]{0:T(1024)S(1)}, f32[2048]{0:T(1024)}, u32[]{:S(2)}) copy-start(f32[2048]{0:T(1024)} %constant.22.clone.symbol_x_ref) | copy-start | bytes 24580
  68.3 61.1 %copy-start.8 = (f32[8]{0:T(128)S(1)}, f32[8]{0:T(128)}, u32[]{:S(2)}) copy-start(f32[8]{0:T(128)} %kz_ref.1) | copy-start | bytes 100

commit v6 on v5

--- a/solution.py
+++ b/solution.py
@@ -113,16 +113,22 @@
 
 
 def x_kernel(outer_ref, section_ref, first_ref, *refs):
-    second_refs, (out_ref, mixed_ref, staged_ref) = refs[:4], refs[4:]
+    second_refs, (out_ref, mixed_ref, places_ref, arrived) = refs[:4], refs[4:]
+    staged_ref = places_ref.reshape(ROOT * PITCH, LANES)
     outer = outer_ref[...]
     zh = lax.axis_index("zh")
+    copies = []
     for dz in range(4):
-        base = ((zh - dz) & 3) * (16 * PITCH)
+        place = places_ref.at[pl.ds(((zh - dz) & 3) * 16, 16), pl.ds(ROWS, ROWS), :]
+        copies.append(pltpu.make_async_copy(second_refs[dz], place, arrived.at[dz]))
+        copies[-1].start()
+    for dz in range(4):
         for xy in range(16):
-            start = pl.multiple_of(base + xy * PITCH, 8)
-            staged_ref[pl.ds(start, ROWS), :] = first_ref[xy, dz]
-            staged_ref[pl.ds(start + ROWS, ROWS), :] = second_refs[dz][xy]
+            places_ref[((zh - dz) & 3) * 16 + xy, :ROWS, :] = first_ref[xy, dz]
     for b in range(0, ROOT, 2):
+        if b == ROWS:
+            for copy in copies:
+                copy.wait()
         pair = jnp.concatenate(
             [staged_ref[pl.ds(b + i, ROOT, stride=PITCH), :] for i in range(2)], axis=1
         )
@@ -160,10 +166,16 @@
 
 def x_transform(first, second):
     outer, sections = x_tables()
+    vmem, whole = pl.BlockSpec(memory_space=pltpu.VMEM), pl.BlockSpec(memory_space=pl.ANY)
     return pl.pallas_call(
         x_kernel,
         out_shape=jax.ShapeDtypeStruct((LENGTH, LANES), jnp.float32),
-        scratch_shapes=[pltpu.VMEM((ROOT * PITCH, LANES), jnp.float32)] * 2,
+        in_specs=[vmem] * 3 + [whole] * 4,
+        scratch_shapes=[
+            pltpu.VMEM((ROOT * PITCH, LANES), jnp.float32),
+            pltpu.VMEM((ROOT, PITCH, LANES), jnp.float32),
+            pltpu.SemaphoreType.DMA((4,)),
+        ],
         compiler_params=LIMIT,
         name="x_transform",
     )(jnp.asarray(outer), jnp.asarray(sections), first, *second)

time: 134 us -> 133 us (level)
  no operation moved by 1% of the time
where the time goes in v6:
time: 133 us
  blocking collectives  99.9 us (75%)
  starting transfers between devices  15.7 us (12%)
  Pallas kernels  7.85 us (6%)
  waiting for transfers between devices  7.49 us (6%)
  local copies, waits for them, and re-layouts  1.83 us (1%)
    all_to_all x1, blocking collectives, body(): lax.all_to_all(spectrum.reshape(256, 16, LANES), AXES, 0, 0, tiled=True)  61.1 us
    all_to_all x2, blocking collectives, across(): lax.all_to_all(v, ('x', 'y'), 0, 0, tiled=True)  38.8 us
    ppermute x6, starting transfers between devices, around(): lax.ppermute(parts[dz], 'zh', [(i, (i + dz) % 4) for i in range(4)])  15.7 us
    ppermute x6, waiting for transfers between devices, around(): lax.ppermute(parts[dz], 'zh', [(i, (i + dz) % 4) for i in range(4)])  7.49 us
    pallas_call x1, Pallas kernels, y_transform(): pl.pallas_call(y_kernel, out_shape=jax.ShapeDtypeStruct((2, 8, PLANES, LE...  4.02 us
  transfers between devices with their start and end apart: 6, of which 1 were waited for; matrix products, arithmetic and copies ran while one was open for 0% of the time, Pallas kernels for 1%

profile of v6, /device:TPU:1, one launch (start us, length us, event | category | flops | bytes accessed | tf_op | source)
XLA Modules:
  0.0 132.9 jit_solution(1629668925463614910)
XLA Ops:
  0.0 1.6 %copy-done.1 = f32[64,8192]{1,0:T(8,128)S(1)} copy-done((f32[64,8192]{1,0:T(8,128)S(1)}, f32[64,8192]{1,0:T(8,128)}, u32[]{:S(2)}) %copy-start.1) | copy-done | bytes 2097176
  1.6 0.3 pack.1
  1.9 3.9 %collective-permute-start = (f32[16,32,128]{2,1,0:T(8,128)S(1)}, f32[16,32,128]{2,1,0:T(8,128)S(1)}, u32[]{:S(2)}, u32[]{:S(2)}) collective-permute-start(f32[16,32,128]{2,1,0:T(8,128)S(1)} %get-tuple-element.27), channel_id=1, source_target_pairs={{0,64},{64,128},{128,192},{192,0},{1,65},{65,129},{129,193},{193,1... | collective-permute-start | bytes 786440 | tf_op jit(solution)/shard_map/ppermute | solution.py:290
  5.8 5.1 %collective-permute-start.1 = (f32[16,32,128]{2,1,0:T(8,128)S(1)}, f32[16,32,128]{2,1,0:T(8,128)S(1)}, u32[]{:S(2)}, u32[]{:S(2)}) collective-permute-start(f32[16,32,128]{2,1,0:T(8,128)S(1)} %get-tuple-element.28), channel_id=1, source_target_pairs={{0,128},{64,192},{128,0},{192,64},{1,129},{65,193},{129,1},{193,65... | collective-permute-start | bytes 786440 | tf_op jit(solution)/shard_map/ppermute | solution.py:290
  10.9 2.4 %collective-permute-start.2 = (f32[16,32,128]{2,1,0:T(8,128)S(1)}, f32[16,32,128]{2,1,0:T(8,128)S(1)}, u32[]{:S(2)}, u32[]{:S(2)}) collective-permute-start(f32[16,32,128]{2,1,0:T(8,128)S(1)} %get-tuple-element.29), channel_id=1, source_target_pairs={{0,192},{64,0},{128,64},{192,128},{1,193},{65,1},{129,65},{193,129... | collective-permute-start | bytes 786440 | tf_op jit(solution)/shard_map/ppermute | solution.py:290
  13.3 21.5 %conditional.2 = (f32[16,4,32,128]{3,2,1,0:T(8,128)S(1)}) conditional(s32[]{:T(128)} %convert_element_type.4, f32[16,4,32,128]{3,2,1,0:T(8,128)S(1)} %get-tuple-element.24, f32[16,4,32,128]{3,2,1,0:T(8,128)S(1)} %get-tuple-element.24), branch_computations={%region_0.0_spmd, %region_1.0_spmd} | conditional | bytes 4194312 | solution.py:296
  13.3 0.1 copy.14
  13.4 21.4 %all_to_all.13 = f32[16,4,32,128]{3,2,1,0:T(8,128)S(1)} all-to-all(f32[16,4,32,128]{3,2,1,0:T(8,128)S(1)} %copy.14), channel_id=1, replica_groups=mesh['zh'=4,'x'=4,'y'=4,'zl'=2,'core'=2] {'x','y'}, dimensions={0} | all-to-all | bytes 2097152 | tf_op jit(solution)/shard_map/cond/branch_1_fun/all_to_all | solution.py:296
  34.7 0.9 split.1
  35.6 1.8 %collective-permute-start.4 = (f32[16,32,128]{2,1,0:T(8,128)}, f32[16,32,128]{2,1,0:T(8,128)}, u32[]{:S(2)}, u32[]{:S(2)}) collective-permute-start(f32[16,32,128]{2,1,0:T(8,128)} %get-tuple-element.31), channel_id=1, source_target_pairs={{0,128},{64,192},{128,0},{192,64},{1,129},{65,193},{129,1},{193,65... | collective-permute-start | bytes 786440 | tf_op jit(solution)/shard_map/ppermute | solution.py:290
  37.4 2.5 %collective-permute-start.5 = (f32[16,32,128]{2,1,0:T(8,128)}, f32[16,32,128]{2,1,0:T(8,128)}, u32[]{:S(2)}, u32[]{:S(2)}) collective-permute-start(f32[16,32,128]{2,1,0:T(8,128)} %get-tuple-element.32), channel_id=1, source_target_pairs={{0,192},{64,0},{128,64},{192,128},{1,193},{65,1},{129,65},{193,129... | collective-permute-start | bytes 786440 | tf_op jit(solution)/shard_map/ppermute | solution.py:290
  40.0 0.1 join.1
  40.0 0.0 copy-start
  40.0 0.0 copy-start.3
  40.1 17.5 %conditional.3 = (f32[16,4,32,128]{3,2,1,0:T(8,128)S(1)}) conditional(s32[]{:T(128)} %convert_element_type.4, f32[16,4,32,128]{3,2,1,0:T(8,128)S(1)} %join.1, f32[16,4,32,128]{3,2,1,0:T(8,128)S(1)} %join.1), branch_computations={%region_2.0_spmd, %region_3.0_spmd} | conditional | bytes 4194312 | solution.py:296
  40.1 0.1 copy.15
  40.2 17.4 %all_to_all.14 = f32[16,4,32,128]{3,2,1,0:T(8,128)S(1)} all-to-all(f32[16,4,32,128]{3,2,1,0:T(8,128)S(1)} %copy.15), channel_id=1, replica_groups=mesh['zh'=4,'x'=4,'y'=4,'zl'=2,'core'=2] {'x','y'}, dimensions={0} | all-to-all | bytes 2097152 | tf_op jit(solution)/shard_map/cond/branch_1_fun/all_to_all | solution.py:296
  57.6 7.5 %collective-permute-done.5.refs_3_ = f32[16,32,128]{2,1,0:T(8,128)} collective-permute-done((f32[16,32,128]{2,1,0:T(8,128)}, f32[16,32,128]{2,1,0:T(8,128)}, u32[]{:S(2)}, u32[]{:S(2)}) %collective-permute-start.5) | collective-permute-done | bytes 262176 | tf_op jit(solution)/shard_map/ppermute | solution.py:290
  65.1 2.6 %x_transform.1 = f32[4096,128]{1,0:T(8,128)S(1)} custom-call(bf16[64,192]{1,0:T(8,128)(2,1)S(1)} %copy-done.3, bf16[33,128,192]{2,1,0:T(8,128)(2,1)S(1)} %copy-done, f32[16,4,32,128]{3,2,1,0:T(8,128)S(1)} %get-tuple-element.34.first_ref, f32[16,32,128]{2,1,0:T(8,128)S(1)} %get-tuple-element.25.earlier_ref.refs_0_, ...), custom_call_target="tpu_custom_call" | custom-call | tf_op jit(solution)/shard_map/x_transform/pallas_call | solution.py:170
  67.7 0.0 copy-start.2
  67.7 0.0 copy-start.5
  67.7 0.0 copy-start.6
  67.7 61.1 %all_to_all.15 = f32[256,16,128]{2,1,0:T(8,128)S(1)} all-to-all(f32[256,16,128]{2,1,0:T(8,128)S(1)} %bitcast.2), channel_id=1, replica_groups=mesh['zh'=4,'x'=4,'y'=4,'zl'=2,'core'=2] {'zh','x','y','zl','core'}, dimensions={0} | all-to-all | bytes 4194304 | tf_op jit(solution)/shard_map/all_to_all | solution.py:306
  128.8 4.0 %y_transform.1 = f32[2,8,8,4096]{3,2,1,0:T(8,128)} custom-call(f32[2048]{0:T(1024)S(1)} %copy-done.7, f32[8]{0:T(128)S(1)} %copy-done.8, bf16[768,512]{1,0:T(8,128)(2,1)S(1)} %copy-done.2, f32[16,256]{1,0:T(8,128)S(1)} %copy-done.6, f32[16,256]{1,0:T(8,128)S(1)} %copy-done.5, f32[16,256]{1,0:T(8,128)S(1)} %copy-done.4, f32[4096,128]{1,0:T(8,128)S(1)} %bitcast.3), custom_call_target="tpu_custom_call" | custom-call | tf_op jit(solution)/shard_map/y_transform/pallas_call | solution.py:264
  (18 shorter events, 0.0 us)
Async XLA Ops:
  0.0 1.6 %copy-start.1 = (f32[64,8192]{1,0:T(8,128)S(1)}, f32[64,8192]{1,0:T(8,128)}, u32[]{:S(2)}) copy-start(f32[64,8192]{1,0:T(8,128)} %density_ref.1) | copy-start | bytes 6291460
  1.9 35.6 %collective-permute-start = (f32[16,32,128]{2,1,0:T(8,128)S(1)}, f32[16,32,128]{2,1,0:T(8,128)S(1)}, u32[]{:S(2)}, u32[]{:S(2)}) collective-permute-start(f32[16,32,128]{2,1,0:T(8,128)S(1)} %get-tuple-element.27), channel_id=1, source_target_pairs={{0,64},{64,128},{128,192},{192,0},{1,65},{65,129},{129,193},{193,1... | collective-permute-start | bytes 786440 | tf_op jit(solution)/shard_map/ppermute | solution.py:290
  5.8 34.2 %collective-permute-start.1 = (f32[16,32,128]{2,1,0:T(8,128)S(1)}, f32[16,32,128]{2,1,0:T(8,128)S(1)}, u32[]{:S(2)}, u32[]{:S(2)}) collective-permute-start(f32[16,32,128]{2,1,0:T(8,128)S(1)} %get-tuple-element.28), channel_id=1, source_target_pairs={{0,128},{64,192},{128,0},{192,64},{1,129},{65,193},{129,1},{193,65... | collective-permute-start | bytes 786440 | tf_op jit(solution)/shard_map/ppermute | solution.py:290
  10.9 29.1 %collective-permute-start.2 = (f32[16,32,128]{2,1,0:T(8,128)S(1)}, f32[16,32,128]{2,1,0:T(8,128)S(1)}, u32[]{:S(2)}, u32[]{:S(2)}) collective-permute-start(f32[16,32,128]{2,1,0:T(8,128)S(1)} %get-tuple-element.29), channel_id=1, source_target_pairs={{0,192},{64,0},{128,64},{192,128},{1,193},{65,1},{129,65},{193,129... | collective-permute-start | bytes 786440 | tf_op jit(solution)/shard_map/ppermute | solution.py:290
  35.6 21.9 %collective-permute-start.3 = (f32[16,32,128]{2,1,0:T(8,128)}, f32[16,32,128]{2,1,0:T(8,128)}, u32[]{:S(2)}, u32[]{:S(2)}) collective-permute-start(f32[16,32,128]{2,1,0:T(8,128)} %get-tuple-element.30), channel_id=1, source_target_pairs={{0,64},{64,128},{128,192},{192,0},{1,65},{65,129},{129,193},{193,1... | collective-permute-start | bytes 786440 | tf_op jit(solution)/shard_map/ppermute | solution.py:290
  35.6 21.9 %collective-permute-start.4 = (f32[16,32,128]{2,1,0:T(8,128)}, f32[16,32,128]{2,1,0:T(8,128)}, u32[]{:S(2)}, u32[]{:S(2)}) collective-permute-start(f32[16,32,128]{2,1,0:T(8,128)} %get-tuple-element.31), channel_id=1, source_target_pairs={{0,128},{64,192},{128,0},{192,64},{1,129},{65,193},{129,1},{193,65... | collective-permute-start | bytes 786440 | tf_op jit(solution)/shard_map/ppermute | solution.py:290
  37.4 27.6 %collective-permute-start.5 = (f32[16,32,128]{2,1,0:T(8,128)}, f32[16,32,128]{2,1,0:T(8,128)}, u32[]{:S(2)}, u32[]{:S(2)}) collective-permute-start(f32[16,32,128]{2,1,0:T(8,128)} %get-tuple-element.32), channel_id=1, source_target_pairs={{0,192},{64,0},{128,64},{192,128},{1,193},{65,1},{129,65},{193,129... | collective-permute-start | bytes 786440 | tf_op jit(solution)/shard_map/ppermute | solution.py:290
  40.0 25.0 %copy-start = (bf16[33,128,192]{2,1,0:T(8,128)(2,1)S(1)}, bf16[33,128,192]{2,1,0:T(8,128)(2,1)}, u32[]{:S(2)}) copy-start(bf16[33,128,192]{2,1,0:T(8,128)(2,1)} %constant.21.clone.section_ref) | copy-start | bytes 4866052
  40.0 25.0 %copy-start.3 = (bf16[64,192]{1,0:T(8,128)(2,1)S(1)}, bf16[64,192]{1,0:T(8,128)(2,1)}, u32[]{:S(2)}) copy-start(bf16[64,192]{1,0:T(8,128)(2,1)} %constant.20.clone.outer_ref) | copy-start | bytes 73732
  67.7 61.1 %copy-start.2 = (bf16[768,512]{1,0:T(8,128)(2,1)S(1)}, bf16[768,512]{1,0:T(8,128)(2,1)}, u32[]{:S(2)}) copy-start(bf16[768,512]{1,0:T(8,128)(2,1)} %constant.23.clone.table_ref) | copy-start | bytes 2359300
  67.7 61.1 %copy-start.4 = (f32[16,256]{1,0:T(8,128)S(1)}, f32[16,256]{1,0:T(8,128)}, u32[]{:S(2)}) copy-start(f32[16,256]{1,0:T(8,128)} %constant.26.clone.symbol_ref) | copy-start | bytes 49156
  67.7 61.1 %copy-start.5 = (f32[16,256]{1,0:T(8,128)S(1)}, f32[16,256]{1,0:T(8,128)}, u32[]{:S(2)}) copy-start(f32[16,256]{1,0:T(8,128)} %constant.25.clone.sine_ref) | copy-start | bytes 49156
  67.7 61.1 %copy-start.6 = (f32[16,256]{1,0:T(8,128)S(1)}, f32[16,256]{1,0:T(8,128)}, u32[]{:S(2)}) copy-start(f32[16,256]{1,0:T(8,128)} %constant.24.clone.cosine_ref) | copy-start | bytes 49156
  67.7 61.1 %copy-start.7 = (f32[2048]{0:T(1024)S(1)}, f32[2048]{0:T(1024)}, u32[]{:S(2)}) copy-start(f32[2048]{0:T(1024)} %constant.22.clone.symbol_x_ref) | copy-start | bytes 24580
  67.7 61.1 %copy-start.8 = (f32[8]{0:T(128)S(1)}, f32[8]{0:T(128)}, u32[]{:S(2)}) copy-start(f32[8]{0:T(128)} %kz_ref.1) | copy-start | bytes 100

commit v7 on v6

--- a/solution.py
+++ b/solution.py
@@ -57,13 +57,15 @@
 def y_tables():
     source = np.arange(256)
     place = (source % 4) * 64 + source // 4
-    angle = 2.0 * np.pi * np.outer(place, np.arange(256)) / 256
-    table = np.concatenate([np.cos(angle), -np.sin(angle)], axis=1)
+    tables = []
+    for odd in range(2):
+        angle = 2.0 * np.pi * np.outer(place[place % 2 == odd], np.arange(LANES)) / 256
+        tables.append(split_table(np.concatenate([np.cos(angle), -np.sin(angle)], axis=1), 0, "hhl"))
     turn = 2.0 * np.pi * np.outer(np.arange(16), np.arange(256)) / LENGTH
     wave = np.arange(LENGTH).reshape(16, 256)
     symbol = 4.0 * np.sin(np.pi * wave / LENGTH) ** 2
     return (
-        split_table(table, 0, "hhl"),
+        np.stack(tables),
         np.cos(turn).astype(np.float32),
         (-np.sin(turn)).astype(np.float32),
         symbol.astype(np.float32),
@@ -217,14 +219,14 @@
 
 
 def y_kernel(symbol_x_ref, kz_ref, table_ref, cosine_ref, sine_ref, symbol_ref, lines_ref, out_ref, done_ref, staged_ref, sent):
-    table = table_ref[...]
     scale = -1.0 / math.sqrt(LENGTH * LENGTH)
     row = lax.broadcasted_iota(jnp.int32, (PLANES, 256), 0)
     kz = jnp.zeros((PLANES, 256), jnp.float32)
     for p in range(PLANES):
         kz = jnp.where(row == p, kz_ref[p], kz)
     for source in range(256):
-        staged_ref[source * 24 : source * 24 + 16, :] = lines_ref[source * 16 : source * 16 + 16, :]
+        at = source // 4 % 2 * 128 + source // 8 * 4 + source % 4
+        staged_ref[at * 24 : at * 24 + 16, :] = lines_ref[source * 16 : source * 16 + 16, :]
     device = 0
     for axis, size in zip(AXES, SIZES):
         device = device * size + lax.axis_index(axis)
@@ -233,14 +235,25 @@
         rows = []
         for part in range(2):
             values = staged_ref[pl.ds(part * 8 + j, 256, stride=24), :]
-            rows.append(split_data(values.T, 1, "hlh"))
-        product = jnp.dot(jnp.concatenate(rows, axis=0), table, preferred_element_type=jnp.float32)
+            rows.append(values.T)
+        lines = jnp.concatenate(rows, axis=0)
+        even, odd = [
+            jnp.dot(
+                split_data(lines[:, i * LANES : (i + 1) * LANES], 1, "hlh"),
+                table_ref[i],
+                preferred_element_type=jnp.float32,
+            )
+            for i in range(2)
+        ]
         values = []
         for n in range(16):
-            first = product[n * 8 : n * 8 + 8]
-            second = product[LANES + n * 8 : LANES + n * 8 + 8]
-            real = first[:, :256] - second[:, 256:]
-            imag = first[:, 256:] + second[:, :256]
+            halves = []
+            for product in (even, odd):
+                first = product[n * 8 : n * 8 + 8]
+                second = product[LANES + n * 8 : LANES + n * 8 + 8]
+                halves.append((first[:, :LANES] - second[:, LANES:], first[:, LANES:] + second[:, :LANES]))
+            total, difference = add(*halves), sub(*halves)
+            real, imag = [jnp.concatenate([total[i], difference[i]], axis=1) for i in range(2)]
             if n:
                 cosine, sine_part = cosine_ref[n : n + 1, :], sine_ref[n : n + 1, :]
                 real, imag = real * cosine - imag * sine_part, imag * cosine + real * sine_part

time: 133 us -> 133 us (level)
  no operation moved by 1% of the time
where the time goes in v7:
time: 133 us; the launch traced here: 132 us
  blocking collectives  99.9 us (75%)
  starting transfers between devices  15.7 us (12%)
  waiting for transfers between devices  7.49 us (6%)
  Pallas kernels  7.43 us (6%)
  local copies, waits for them, and re-layouts  1.83 us (1%)
    all_to_all x1, blocking collectives, body(): lax.all_to_all(spectrum.reshape(256, 16, LANES), AXES, 0, 0, tiled=True)  61.1 us
    all_to_all x2, blocking collectives, across(): lax.all_to_all(v, ('x', 'y'), 0, 0, tiled=True)  38.8 us
    ppermute x6, starting transfers between devices, around(): lax.ppermute(parts[dz], 'zh', [(i, (i + dz) % 4) for i in range(4)])  15.7 us
    ppermute x6, waiting for transfers between devices, around(): lax.ppermute(parts[dz], 'zh', [(i, (i + dz) % 4) for i in range(4)])  7.49 us
    pallas_call x1, Pallas kernels, y_transform(): pl.pallas_call(y_kernel, out_shape=jax.ShapeDtypeStruct((2, 8, PLANES, LE...  3.6 us
  transfers between devices with their start and end apart: 6, of which 1 were waited for; matrix products, arithmetic and copies ran while one was open for 0% of the time, Pallas kernels for 1%

profile of v7, /device:TPU:1, one launch (start us, length us, event | category | flops | bytes accessed | tf_op | source)
XLA Modules:
  0.0 132.4 jit_solution(1174257569594722127)
XLA Ops:
  0.0 1.6 %copy-done.1 = f32[64,8192]{1,0:T(8,128)S(1)} copy-done((f32[64,8192]{1,0:T(8,128)S(1)}, f32[64,8192]{1,0:T(8,128)}, u32[]{:S(2)}) %copy-start.1) | copy-done | bytes 2097176
  1.6 0.3 pack.1
  1.9 3.9 %collective-permute-start = (f32[16,32,128]{2,1,0:T(8,128)S(1)}, f32[16,32,128]{2,1,0:T(8,128)S(1)}, u32[]{:S(2)}, u32[]{:S(2)}) collective-permute-start(f32[16,32,128]{2,1,0:T(8,128)S(1)} %get-tuple-element.27), channel_id=1, source_target_pairs={{0,64},{64,128},{128,192},{192,0},{1,65},{65,129},{129,193},{193,1... | collective-permute-start | bytes 786440 | tf_op jit(solution)/shard_map/ppermute | solution.py:303
  5.8 5.1 %collective-permute-start.1 = (f32[16,32,128]{2,1,0:T(8,128)S(1)}, f32[16,32,128]{2,1,0:T(8,128)S(1)}, u32[]{:S(2)}, u32[]{:S(2)}) collective-permute-start(f32[16,32,128]{2,1,0:T(8,128)S(1)} %get-tuple-element.28), channel_id=1, source_target_pairs={{0,128},{64,192},{128,0},{192,64},{1,129},{65,193},{129,1},{193,65... | collective-permute-start | bytes 786440 | tf_op jit(solution)/shard_map/ppermute | solution.py:303
  10.9 2.4 %collective-permute-start.2 = (f32[16,32,128]{2,1,0:T(8,128)S(1)}, f32[16,32,128]{2,1,0:T(8,128)S(1)}, u32[]{:S(2)}, u32[]{:S(2)}) collective-permute-start(f32[16,32,128]{2,1,0:T(8,128)S(1)} %get-tuple-element.29), channel_id=1, source_target_pairs={{0,192},{64,0},{128,64},{192,128},{1,193},{65,1},{129,65},{193,129... | collective-permute-start | bytes 786440 | tf_op jit(solution)/shard_map/ppermute | solution.py:303
  13.3 21.5 %conditional.2 = (f32[16,4,32,128]{3,2,1,0:T(8,128)S(1)}) conditional(s32[]{:T(128)} %convert_element_type.4, f32[16,4,32,128]{3,2,1,0:T(8,128)S(1)} %get-tuple-element.24, f32[16,4,32,128]{3,2,1,0:T(8,128)S(1)} %get-tuple-element.24), branch_computations={%region_0.0_spmd, %region_1.0_spmd} | conditional | bytes 4194312 | solution.py:309
  13.3 0.1 copy.14
  13.4 21.4 %all_to_all.13 = f32[16,4,32,128]{3,2,1,0:T(8,128)S(1)} all-to-all(f32[16,4,32,128]{3,2,1,0:T(8,128)S(1)} %copy.14), channel_id=1, replica_groups=mesh['zh'=4,'x'=4,'y'=4,'zl'=2,'core'=2] {'x','y'}, dimensions={0} | all-to-all | bytes 2097152 | tf_op jit(solution)/shard_map/cond/branch_1_fun/all_to_all | solution.py:309
  34.7 0.9 split.1
  35.6 1.8 %collective-permute-start.4 = (f32[16,32,128]{2,1,0:T(8,128)}, f32[16,32,128]{2,1,0:T(8,128)}, u32[]{:S(2)}, u32[]{:S(2)}) collective-permute-start(f32[16,32,128]{2,1,0:T(8,128)} %get-tuple-element.31), channel_id=1, source_target_pairs={{0,128},{64,192},{128,0},{192,64},{1,129},{65,193},{129,1},{193,65... | collective-permute-start | bytes 786440 | tf_op jit(solution)/shard_map/ppermute | solution.py:303
  37.4 2.5 %collective-permute-start.5 = (f32[16,32,128]{2,1,0:T(8,128)}, f32[16,32,128]{2,1,0:T(8,128)}, u32[]{:S(2)}, u32[]{:S(2)}) collective-permute-start(f32[16,32,128]{2,1,0:T(8,128)} %get-tuple-element.32), channel_id=1, source_target_pairs={{0,192},{64,0},{128,64},{192,128},{1,193},{65,1},{129,65},{193,129... | collective-permute-start | bytes 786440 | tf_op jit(solution)/shard_map/ppermute | solution.py:303
  40.0 0.1 join.1
  40.0 0.0 copy-start
  40.0 0.0 copy-start.3
  40.1 17.5 %conditional.3 = (f32[16,4,32,128]{3,2,1,0:T(8,128)S(1)}) conditional(s32[]{:T(128)} %convert_element_type.4, f32[16,4,32,128]{3,2,1,0:T(8,128)S(1)} %join.1, f32[16,4,32,128]{3,2,1,0:T(8,128)S(1)} %join.1), branch_computations={%region_2.0_spmd, %region_3.0_spmd} | conditional | bytes 4194312 | solution.py:309
  40.1 0.1 copy.15
  40.2 17.4 %all_to_all.14 = f32[16,4,32,128]{3,2,1,0:T(8,128)S(1)} all-to-all(f32[16,4,32,128]{3,2,1,0:T(8,128)S(1)} %copy.15), channel_id=1, replica_groups=mesh['zh'=4,'x'=4,'y'=4,'zl'=2,'core'=2] {'x','y'}, dimensions={0} | all-to-all | bytes 2097152 | tf_op jit(solution)/shard_map/cond/branch_1_fun/all_to_all | solution.py:309
  57.6 7.5 %collective-permute-done.5.refs_3_ = f32[16,32,128]{2,1,0:T(8,128)} collective-permute-done((f32[16,32,128]{2,1,0:T(8,128)}, f32[16,32,128]{2,1,0:T(8,128)}, u32[]{:S(2)}, u32[]{:S(2)}) %collective-permute-start.5) | collective-permute-done | bytes 262176 | tf_op jit(solution)/shard_map/ppermute | solution.py:303
  65.1 2.6 %x_transform.1 = f32[4096,128]{1,0:T(8,128)S(1)} custom-call(bf16[64,192]{1,0:T(8,128)(2,1)S(1)} %copy-done.3, bf16[33,128,192]{2,1,0:T(8,128)(2,1)S(1)} %copy-done, f32[16,4,32,128]{3,2,1,0:T(8,128)S(1)} %get-tuple-element.34.first_ref, f32[16,32,128]{2,1,0:T(8,128)S(1)} %get-tuple-element.25.earlier_ref.refs_0_, ...), custom_call_target="tpu_custom_call" | custom-call | tf_op jit(solution)/shard_map/x_transform/pallas_call | solution.py:172
  67.7 0.0 copy-start.2
  67.7 0.0 copy-start.5
  67.7 0.0 copy-start.6
  67.7 61.1 %all_to_all.15 = f32[256,16,128]{2,1,0:T(8,128)S(1)} all-to-all(f32[256,16,128]{2,1,0:T(8,128)S(1)} %bitcast.2), channel_id=1, replica_groups=mesh['zh'=4,'x'=4,'y'=4,'zl'=2,'core'=2] {'zh','x','y','zl','core'}, dimensions={0} | all-to-all | bytes 4194304 | tf_op jit(solution)/shard_map/all_to_all | solution.py:319
  128.8 3.6 %y_transform.1 = f32[2,8,8,4096]{3,2,1,0:T(8,128)} custom-call(f32[2048]{0:T(1024)S(1)} %copy-done.7, f32[8]{0:T(128)S(1)} %copy-done.8, bf16[2,384,256]{2,1,0:T(8,128)(2,1)S(1)} %copy-done.2, f32[16,256]{1,0:T(8,128)S(1)} %copy-done.6, f32[16,256]{1,0:T(8,128)S(1)} %copy-done.5, f32[16,256]{1,0:T(8,128)S(1)} %copy-done.4, f32[4096,128]{1,0:T(8,128)S(1)} %bitcast.3), custom_call_target="tpu_custom_call" | custom-call | tf_op jit(solution)/shard_map/y_transform/pallas_call | solution.py:277
  (18 shorter events, 0.0 us)
Async XLA Ops:
  0.0 1.6 %copy-start.1 = (f32[64,8192]{1,0:T(8,128)S(1)}, f32[64,8192]{1,0:T(8,128)}, u32[]{:S(2)}) copy-start(f32[64,8192]{1,0:T(8,128)} %density_ref.1) | copy-start | bytes 6291460
  1.9 35.6 %collective-permute-start = (f32[16,32,128]{2,1,0:T(8,128)S(1)}, f32[16,32,128]{2,1,0:T(8,128)S(1)}, u32[]{:S(2)}, u32[]{:S(2)}) collective-permute-start(f32[16,32,128]{2,1,0:T(8,128)S(1)} %get-tuple-element.27), channel_id=1, source_target_pairs={{0,64},{64,128},{128,192},{192,0},{1,65},{65,129},{129,193},{193,1... | collective-permute-start | bytes 786440 | tf_op jit(solution)/shard_map/ppermute | solution.py:303
  5.8 34.2 %collective-permute-start.1 = (f32[16,32,128]{2,1,0:T(8,128)S(1)}, f32[16,32,128]{2,1,0:T(8,128)S(1)}, u32[]{:S(2)}, u32[]{:S(2)}) collective-permute-start(f32[16,32,128]{2,1,0:T(8,128)S(1)} %get-tuple-element.28), channel_id=1, source_target_pairs={{0,128},{64,192},{128,0},{192,64},{1,129},{65,193},{129,1},{193,65... | collective-permute-start | bytes 786440 | tf_op jit(solution)/shard_map/ppermute | solution.py:303
  10.9 29.1 %collective-permute-start.2 = (f32[16,32,128]{2,1,0:T(8,128)S(1)}, f32[16,32,128]{2,1,0:T(8,128)S(1)}, u32[]{:S(2)}, u32[]{:S(2)}) collective-permute-start(f32[16,32,128]{2,1,0:T(8,128)S(1)} %get-tuple-element.29), channel_id=1, source_target_pairs={{0,192},{64,0},{128,64},{192,128},{1,193},{65,1},{129,65},{193,129... | collective-permute-start | bytes 786440 | tf_op jit(solution)/shard_map/ppermute | solution.py:303
  35.6 21.9 %collective-permute-start.3 = (f32[16,32,128]{2,1,0:T(8,128)}, f32[16,32,128]{2,1,0:T(8,128)}, u32[]{:S(2)}, u32[]{:S(2)}) collective-permute-start(f32[16,32,128]{2,1,0:T(8,128)} %get-tuple-element.30), channel_id=1, source_target_pairs={{0,64},{64,128},{128,192},{192,0},{1,65},{65,129},{129,193},{193,1... | collective-permute-start | bytes 786440 | tf_op jit(solution)/shard_map/ppermute | solution.py:303
  35.6 21.9 %collective-permute-start.4 = (f32[16,32,128]{2,1,0:T(8,128)}, f32[16,32,128]{2,1,0:T(8,128)}, u32[]{:S(2)}, u32[]{:S(2)}) collective-permute-start(f32[16,32,128]{2,1,0:T(8,128)} %get-tuple-element.31), channel_id=1, source_target_pairs={{0,128},{64,192},{128,0},{192,64},{1,129},{65,193},{129,1},{193,65... | collective-permute-start | bytes 786440 | tf_op jit(solution)/shard_map/ppermute | solution.py:303
  37.4 27.6 %collective-permute-start.5 = (f32[16,32,128]{2,1,0:T(8,128)}, f32[16,32,128]{2,1,0:T(8,128)}, u32[]{:S(2)}, u32[]{:S(2)}) collective-permute-start(f32[16,32,128]{2,1,0:T(8,128)} %get-tuple-element.32), channel_id=1, source_target_pairs={{0,192},{64,0},{128,64},{192,128},{1,193},{65,1},{129,65},{193,129... | collective-permute-start | bytes 786440 | tf_op jit(solution)/shard_map/ppermute | solution.py:303
  40.0 25.0 %copy-start = (bf16[33,128,192]{2,1,0:T(8,128)(2,1)S(1)}, bf16[33,128,192]{2,1,0:T(8,128)(2,1)}, u32[]{:S(2)}) copy-start(bf16[33,128,192]{2,1,0:T(8,128)(2,1)} %constant.21.clone.section_ref) | copy-start | bytes 4866052
  40.0 25.0 %copy-start.3 = (bf16[64,192]{1,0:T(8,128)(2,1)S(1)}, bf16[64,192]{1,0:T(8,128)(2,1)}, u32[]{:S(2)}) copy-start(bf16[64,192]{1,0:T(8,128)(2,1)} %constant.20.clone.outer_ref) | copy-start | bytes 73732
  67.7 61.1 %copy-start.2 = (bf16[2,384,256]{2,1,0:T(8,128)(2,1)S(1)}, bf16[2,384,256]{2,1,0:T(8,128)(2,1)}, u32[]{:S(2)}) copy-start(bf16[2,384,256]{2,1,0:T(8,128)(2,1)} %constant.23.clone.table_ref) | copy-start | bytes 1179652
  67.7 61.1 %copy-start.4 = (f32[16,256]{1,0:T(8,128)S(1)}, f32[16,256]{1,0:T(8,128)}, u32[]{:S(2)}) copy-start(f32[16,256]{1,0:T(8,128)} %constant.26.clone.symbol_ref) | copy-start | bytes 49156
  67.7 61.1 %copy-start.5 = (f32[16,256]{1,0:T(8,128)S(1)}, f32[16,256]{1,0:T(8,128)}, u32[]{:S(2)}) copy-start(f32[16,256]{1,0:T(8,128)} %constant.25.clone.sine_ref) | copy-start | bytes 49156
  67.7 61.1 %copy-start.6 = (f32[16,256]{1,0:T(8,128)S(1)}, f32[16,256]{1,0:T(8,128)}, u32[]{:S(2)}) copy-start(f32[16,256]{1,0:T(8,128)} %constant.24.clone.cosine_ref) | copy-start | bytes 49156
  67.7 61.1 %copy-start.7 = (f32[2048]{0:T(1024)S(1)}, f32[2048]{0:T(1024)}, u32[]{:S(2)}) copy-start(f32[2048]{0:T(1024)} %constant.22.clone.symbol_x_ref) | copy-start | bytes 24580
  67.7 61.1 %copy-start.8 = (f32[8]{0:T(128)S(1)}, f32[8]{0:T(128)}, u32[]{:S(2)}) copy-start(f32[8]{0:T(128)} %kz_ref.1) | copy-start | bytes 100

commit v8 on v7

--- a/solution.py
+++ b/solution.py
@@ -230,6 +230,7 @@
     device = 0
     for axis, size in zip(AXES, SIZES):
         device = device * size + lax.axis_index(axis)
+    symbol_x = symbol_x_ref[pl.ds(device, 1), :]
     copies = []
     for j in range(8):
         rows = []
@@ -258,13 +259,16 @@
                 cosine, sine_part = cosine_ref[n : n + 1, :], sine_ref[n : n + 1, :]
                 real, imag = real * cosine - imag * sine_part, imag * cosine + real * sine_part
             values.append((real, imag))
-        shift = kz + symbol_x_ref[device * 8 + j]
+        shift = kz + symbol_x[:, j : j + 1]
         for k, (real, imag) in enumerate(sixteen(values)):
             factor = scale / (shift + symbol_ref[k : k + 1, :])
             done_ref[j, 0, :, k * 256 : (k + 1) * 256] = real * factor
             done_ref[j, 1, :, k * 256 : (k + 1) * 256] = imag * factor
-        copies.append(pltpu.make_async_copy(done_ref.at[j], out_ref.at[:, j], sent.at[j]))
-        copies[-1].start()
+            if k == 15 or (j, k) == (7, 7):
+                part = pl.ds(2048 * (k // 15), 2048) if j == 7 else pl.ds(0, LENGTH)
+                source, target = done_ref.at[j, :, :, part], out_ref.at[:, j, :, part]
+                copies.append(pltpu.make_async_copy(source, target, sent.at[len(copies)]))
+                copies[-1].start()
     for copy in copies:
         copy.wait()
 
@@ -272,17 +276,18 @@
 def y_transform(lines, kz_square):
     table, cosine, sine_part, symbol = y_tables()
     symbol_x = (4.0 * np.sin(np.pi * np.arange(KEPT) / LENGTH) ** 2).astype(np.float32)
+    symbol_x = np.pad(symbol_x.reshape(256, 8), ((0, 0), (0, LANES - 8)))
     vmem = pl.BlockSpec(memory_space=pltpu.VMEM)
     smem = pl.BlockSpec(memory_space=pltpu.SMEM)
     return pl.pallas_call(
         y_kernel,
         out_shape=jax.ShapeDtypeStruct((2, 8, PLANES, LENGTH), jnp.float32),
-        in_specs=[smem] * 2 + [vmem] * 5,
+        in_specs=[vmem, smem] + [vmem] * 5,
         out_specs=pl.BlockSpec(memory_space=pl.ANY),
         scratch_shapes=[
             pltpu.VMEM((8, 2, PLANES, LENGTH), jnp.float32),
             pltpu.VMEM((256 * 24, LANES), jnp.float32),
-            pltpu.SemaphoreType.DMA((8,)),
+            pltpu.SemaphoreType.DMA((9,)),
         ],
         compiler_params=LIMIT,
         name="y_transform",

time: 133 us -> 133 us (level)
  no operation moved by 1% of the time
where the time goes in v8:
time: 133 us; the launch traced here: 132 us
  blocking collectives  99.9 us (75%)
  starting transfers between devices  15.7 us (12%)
  waiting for transfers between devices  7.49 us (6%)
  Pallas kernels  7.38 us (6%)
  local copies, waits for them, and re-layouts  1.83 us (1%)
    all_to_all x1, blocking collectives, body(): lax.all_to_all(spectrum.reshape(256, 16, LANES), AXES, 0, 0, tiled=True)  61.1 us
    all_to_all x2, blocking collectives, across(): lax.all_to_all(v, ('x', 'y'), 0, 0, tiled=True)  38.8 us
    ppermute x6, starting transfers between devices, around(): lax.ppermute(parts[dz], 'zh', [(i, (i + dz) % 4) for i in range(4)])  15.7 us
    ppermute x6, waiting for transfers between devices, around(): lax.ppermute(parts[dz], 'zh', [(i, (i + dz) % 4) for i in range(4)])  7.49 us
    pallas_call x1, Pallas kernels, y_transform(): pl.pallas_call(y_kernel, out_shape=jax.ShapeDtypeStruct((2, 8, PLANES, LE...  3.55 us
  transfers between devices with their start and end apart: 6, of which 1 were waited for; matrix products, arithmetic and copies ran while one was open for 0% of the time, Pallas kernels for 1%

profile of v8, /device:TPU:1, one launch (start us, length us, event | category | flops | bytes accessed | tf_op | source)
XLA Modules:
  0.0 132.4 jit_solution(12730384339504946783)
XLA Ops:
  0.0 1.6 %copy-done.1 = f32[64,8192]{1,0:T(8,128)S(1)} copy-done((f32[64,8192]{1,0:T(8,128)S(1)}, f32[64,8192]{1,0:T(8,128)}, u32[]{:S(2)}) %copy-start.1) | copy-done | bytes 2097176
  1.6 0.3 pack.1
  1.9 3.9 %collective-permute-start = (f32[16,32,128]{2,1,0:T(8,128)S(1)}, f32[16,32,128]{2,1,0:T(8,128)S(1)}, u32[]{:S(2)}, u32[]{:S(2)}) collective-permute-start(f32[16,32,128]{2,1,0:T(8,128)S(1)} %get-tuple-element.27), channel_id=1, source_target_pairs={{0,64},{64,128},{128,192},{192,0},{1,65},{65,129},{129,193},{193,1... | collective-permute-start | bytes 786440 | tf_op jit(solution)/shard_map/ppermute | solution.py:308
  5.8 5.1 %collective-permute-start.1 = (f32[16,32,128]{2,1,0:T(8,128)S(1)}, f32[16,32,128]{2,1,0:T(8,128)S(1)}, u32[]{:S(2)}, u32[]{:S(2)}) collective-permute-start(f32[16,32,128]{2,1,0:T(8,128)S(1)} %get-tuple-element.28), channel_id=1, source_target_pairs={{0,128},{64,192},{128,0},{192,64},{1,129},{65,193},{129,1},{193,65... | collective-permute-start | bytes 786440 | tf_op jit(solution)/shard_map/ppermute | solution.py:308
  10.9 2.4 %collective-permute-start.2 = (f32[16,32,128]{2,1,0:T(8,128)S(1)}, f32[16,32,128]{2,1,0:T(8,128)S(1)}, u32[]{:S(2)}, u32[]{:S(2)}) collective-permute-start(f32[16,32,128]{2,1,0:T(8,128)S(1)} %get-tuple-element.29), channel_id=1, source_target_pairs={{0,192},{64,0},{128,64},{192,128},{1,193},{65,1},{129,65},{193,129... | collective-permute-start | bytes 786440 | tf_op jit(solution)/shard_map/ppermute | solution.py:308
  13.3 21.5 %conditional.2 = (f32[16,4,32,128]{3,2,1,0:T(8,128)S(1)}) conditional(s32[]{:T(128)} %convert_element_type.4, f32[16,4,32,128]{3,2,1,0:T(8,128)S(1)} %get-tuple-element.24, f32[16,4,32,128]{3,2,1,0:T(8,128)S(1)} %get-tuple-element.24), branch_computations={%region_0.0_spmd, %region_1.0_spmd} | conditional | bytes 4194312 | solution.py:314
  13.3 0.1 copy.14
  13.4 21.4 %all_to_all.13 = f32[16,4,32,128]{3,2,1,0:T(8,128)S(1)} all-to-all(f32[16,4,32,128]{3,2,1,0:T(8,128)S(1)} %copy.14), channel_id=1, replica_groups=mesh['zh'=4,'x'=4,'y'=4,'zl'=2,'core'=2] {'x','y'}, dimensions={0} | all-to-all | bytes 2097152 | tf_op jit(solution)/shard_map/cond/branch_1_fun/all_to_all | solution.py:314
  34.7 0.9 split.1
  35.6 1.8 %collective-permute-start.4 = (f32[16,32,128]{2,1,0:T(8,128)}, f32[16,32,128]{2,1,0:T(8,128)}, u32[]{:S(2)}, u32[]{:S(2)}) collective-permute-start(f32[16,32,128]{2,1,0:T(8,128)} %get-tuple-element.31), channel_id=1, source_target_pairs={{0,128},{64,192},{128,0},{192,64},{1,129},{65,193},{129,1},{193,65... | collective-permute-start | bytes 786440 | tf_op jit(solution)/shard_map/ppermute | solution.py:308
  37.4 2.5 %collective-permute-start.5 = (f32[16,32,128]{2,1,0:T(8,128)}, f32[16,32,128]{2,1,0:T(8,128)}, u32[]{:S(2)}, u32[]{:S(2)}) collective-permute-start(f32[16,32,128]{2,1,0:T(8,128)} %get-tuple-element.32), channel_id=1, source_target_pairs={{0,192},{64,0},{128,64},{192,128},{1,193},{65,1},{129,65},{193,129... | collective-permute-start | bytes 786440 | tf_op jit(solution)/shard_map/ppermute | solution.py:308
  40.0 0.1 join.1
  40.0 0.0 copy-start
  40.0 0.0 copy-start.4
  40.1 17.5 %conditional.3 = (f32[16,4,32,128]{3,2,1,0:T(8,128)S(1)}) conditional(s32[]{:T(128)} %convert_element_type.4, f32[16,4,32,128]{3,2,1,0:T(8,128)S(1)} %join.1, f32[16,4,32,128]{3,2,1,0:T(8,128)S(1)} %join.1), branch_computations={%region_2.0_spmd, %region_3.0_spmd} | conditional | bytes 4194312 | solution.py:314
  40.1 0.1 copy.15
  40.2 17.4 %all_to_all.14 = f32[16,4,32,128]{3,2,1,0:T(8,128)S(1)} all-to-all(f32[16,4,32,128]{3,2,1,0:T(8,128)S(1)} %copy.15), channel_id=1, replica_groups=mesh['zh'=4,'x'=4,'y'=4,'zl'=2,'core'=2] {'x','y'}, dimensions={0} | all-to-all | bytes 2097152 | tf_op jit(solution)/shard_map/cond/branch_1_fun/all_to_all | solution.py:314
  57.6 7.5 %collective-permute-done.5.refs_3_ = f32[16,32,128]{2,1,0:T(8,128)} collective-permute-done((f32[16,32,128]{2,1,0:T(8,128)}, f32[16,32,128]{2,1,0:T(8,128)}, u32[]{:S(2)}, u32[]{:S(2)}) %collective-permute-start.5) | collective-permute-done | bytes 262176 | tf_op jit(solution)/shard_map/ppermute | solution.py:308
  65.1 2.6 %x_transform.1 = f32[4096,128]{1,0:T(8,128)S(1)} custom-call(bf16[64,192]{1,0:T(8,128)(2,1)S(1)} %copy-done.4, bf16[33,128,192]{2,1,0:T(8,128)(2,1)S(1)} %copy-done, f32[16,4,32,128]{3,2,1,0:T(8,128)S(1)} %get-tuple-element.34.first_ref, f32[16,32,128]{2,1,0:T(8,128)S(1)} %get-tuple-element.25.earlier_ref.refs_0_, ...), custom_call_target="tpu_custom_call" | custom-call | tf_op jit(solution)/shard_map/x_transform/pallas_call | solution.py:172
  67.7 0.0 copy-start.2
  67.7 0.0 copy-start.3
  67.7 0.0 copy-start.6
  67.7 61.1 %all_to_all.15 = f32[256,16,128]{2,1,0:T(8,128)S(1)} all-to-all(f32[256,16,128]{2,1,0:T(8,128)S(1)} %bitcast.2), channel_id=1, replica_groups=mesh['zh'=4,'x'=4,'y'=4,'zl'=2,'core'=2] {'zh','x','y','zl','core'}, dimensions={0} | all-to-all | bytes 4194304 | tf_op jit(solution)/shard_map/all_to_all | solution.py:324
  128.8 3.6 %y_transform.1 = f32[2,8,8,4096]{3,2,1,0:T(8,128)} custom-call(f32[256,128]{1,0:T(8,128)S(1)} %copy-done.3, f32[8]{0:T(128)S(1)} %copy-done.8, bf16[2,384,256]{2,1,0:T(8,128)(2,1)S(1)} %copy-done.2, f32[16,256]{1,0:T(8,128)S(1)} %copy-done.7, f32[16,256]{1,0:T(8,128)S(1)} %copy-done.6, f32[16,256]{1,0:T(8,128)S(1)} %copy-done.5, f32[4096,128]{1,0:T(8,128)S(1)} %bitcast.3), custom_call_target="tpu_custom_call" | custom-call | tf_op jit(solution)/shard_map/y_transform/pallas_call | solution.py:282
  (18 shorter events, 0.0 us)
Async XLA Ops:
  0.0 1.6 %copy-start.1 = (f32[64,8192]{1,0:T(8,128)S(1)}, f32[64,8192]{1,0:T(8,128)}, u32[]{:S(2)}) copy-start(f32[64,8192]{1,0:T(8,128)} %density_ref.1) | copy-start | bytes 6291460
  1.9 35.6 %collective-permute-start = (f32[16,32,128]{2,1,0:T(8,128)S(1)}, f32[16,32,128]{2,1,0:T(8,128)S(1)}, u32[]{:S(2)}, u32[]{:S(2)}) collective-permute-start(f32[16,32,128]{2,1,0:T(8,128)S(1)} %get-tuple-element.27), channel_id=1, source_target_pairs={{0,64},{64,128},{128,192},{192,0},{1,65},{65,129},{129,193},{193,1... | collective-permute-start | bytes 786440 | tf_op jit(solution)/shard_map/ppermute | solution.py:308
  5.8 34.2 %collective-permute-start.1 = (f32[16,32,128]{2,1,0:T(8,128)S(1)}, f32[16,32,128]{2,1,0:T(8,128)S(1)}, u32[]{:S(2)}, u32[]{:S(2)}) collective-permute-start(f32[16,32,128]{2,1,0:T(8,128)S(1)} %get-tuple-element.28), channel_id=1, source_target_pairs={{0,128},{64,192},{128,0},{192,64},{1,129},{65,193},{129,1},{193,65... | collective-permute-start | bytes 786440 | tf_op jit(solution)/shard_map/ppermute | solution.py:308
  10.9 29.1 %collective-permute-start.2 = (f32[16,32,128]{2,1,0:T(8,128)S(1)}, f32[16,32,128]{2,1,0:T(8,128)S(1)}, u32[]{:S(2)}, u32[]{:S(2)}) collective-permute-start(f32[16,32,128]{2,1,0:T(8,128)S(1)} %get-tuple-element.29), channel_id=1, source_target_pairs={{0,192},{64,0},{128,64},{192,128},{1,193},{65,1},{129,65},{193,129... | collective-permute-start | bytes 786440 | tf_op jit(solution)/shard_map/ppermute | solution.py:308
  35.6 21.9 %collective-permute-start.3 = (f32[16,32,128]{2,1,0:T(8,128)}, f32[16,32,128]{2,1,0:T(8,128)}, u32[]{:S(2)}, u32[]{:S(2)}) collective-permute-start(f32[16,32,128]{2,1,0:T(8,128)} %get-tuple-element.30), channel_id=1, source_target_pairs={{0,64},{64,128},{128,192},{192,0},{1,65},{65,129},{129,193},{193,1... | collective-permute-start | bytes 786440 | tf_op jit(solution)/shard_map/ppermute | solution.py:308
  35.6 21.9 %collective-permute-start.4 = (f32[16,32,128]{2,1,0:T(8,128)}, f32[16,32,128]{2,1,0:T(8,128)}, u32[]{:S(2)}, u32[]{:S(2)}) collective-permute-start(f32[16,32,128]{2,1,0:T(8,128)} %get-tuple-element.31), channel_id=1, source_target_pairs={{0,128},{64,192},{128,0},{192,64},{1,129},{65,193},{129,1},{193,65... | collective-permute-start | bytes 786440 | tf_op jit(solution)/shard_map/ppermute | solution.py:308
  37.4 27.6 %collective-permute-start.5 = (f32[16,32,128]{2,1,0:T(8,128)}, f32[16,32,128]{2,1,0:T(8,128)}, u32[]{:S(2)}, u32[]{:S(2)}) collective-permute-start(f32[16,32,128]{2,1,0:T(8,128)} %get-tuple-element.32), channel_id=1, source_target_pairs={{0,192},{64,0},{128,64},{192,128},{1,193},{65,1},{129,65},{193,129... | collective-permute-start | bytes 786440 | tf_op jit(solution)/shard_map/ppermute | solution.py:308
  40.0 25.0 %copy-start = (bf16[33,128,192]{2,1,0:T(8,128)(2,1)S(1)}, bf16[33,128,192]{2,1,0:T(8,128)(2,1)}, u32[]{:S(2)}) copy-start(bf16[33,128,192]{2,1,0:T(8,128)(2,1)} %constant.21.clone.section_ref) | copy-start | bytes 4866052
  40.0 25.0 %copy-start.4 = (bf16[64,192]{1,0:T(8,128)(2,1)S(1)}, bf16[64,192]{1,0:T(8,128)(2,1)}, u32[]{:S(2)}) copy-start(bf16[64,192]{1,0:T(8,128)(2,1)} %constant.20.clone.outer_ref) | copy-start | bytes 73732
  67.7 61.1 %copy-start.2 = (bf16[2,384,256]{2,1,0:T(8,128)(2,1)S(1)}, bf16[2,384,256]{2,1,0:T(8,128)(2,1)}, u32[]{:S(2)}) copy-start(bf16[2,384,256]{2,1,0:T(8,128)(2,1)} %constant.23.clone.table_ref) | copy-start | bytes 1179652
  67.7 61.1 %copy-start.3 = (f32[256,128]{1,0:T(8,128)S(1)}, f32[256,128]{1,0:T(8,128)}, u32[]{:S(2)}) copy-start(f32[256,128]{1,0:T(8,128)} %constant.22.clone.symbol_x_ref) | copy-start | bytes 393220
  67.7 61.1 %copy-start.5 = (f32[16,256]{1,0:T(8,128)S(1)}, f32[16,256]{1,0:T(8,128)}, u32[]{:S(2)}) copy-start(f32[16,256]{1,0:T(8,128)} %constant.26.clone.symbol_ref) | copy-start | bytes 49156
  67.7 61.1 %copy-start.6 = (f32[16,256]{1,0:T(8,128)S(1)}, f32[16,256]{1,0:T(8,128)}, u32[]{:S(2)}) copy-start(f32[16,256]{1,0:T(8,128)} %constant.25.clone.sine_ref) | copy-start | bytes 49156
  67.7 61.1 %copy-start.7 = (f32[16,256]{1,0:T(8,128)S(1)}, f32[16,256]{1,0:T(8,128)}, u32[]{:S(2)}) copy-start(f32[16,256]{1,0:T(8,128)} %constant.24.clone.cosine_ref) | copy-start | bytes 49156
  67.7 61.1 %copy-start.8 = (f32[8]{0:T(128)S(1)}, f32[8]{0:T(128)}, u32[]{:S(2)}) copy-start(f32[8]{0:T(128)} %kz_ref.1) | copy-start | bytes 100
